TPU v7x, 128 devices: a whole 4x4x4 slice. The times are simulated.
128 devices in a mesh: branch: 4 (over x_hi, core), fsdp: 32 (over x_lo, z, y).
Axes of the slice: x: 4 (x_hi: 2, x_lo: 2; x = x_hi * 2 + x_lo), y: 4, z: 4, core: 2. Of those that a mesh axis runs over, the one named last changes fastest.
Arguments:
- attention_out: bfloat16 [4, 4096, 4096], P('branch', 'fsdp'), may hold values from -0.09375 to 0.09375
- tokens: bfloat16 [1024, 4096], P('fsdp', 'branch'), may hold values from -6 to 6
- out_grads: bfloat16 [1024, 4096], P('fsdp', 'branch'), may hold values from -6 to 6
- route_ids: int32 [1024, 2], P('fsdp'), may hold values from 0 to 3, all different within a row; in each aligned block of 32 rows (0 to 31, 32 to 63, ...) at most 18 rows name the same one
- route_gates: float32 [1024, 2], P('fsdp'), may hold values from 0.2 to 1
- gate_weight: bfloat16 [4, 4096, 11008], P('branch', 'fsdp'), may hold values from -0.09375 to 0.09375
- up_weight: bfloat16 [4, 4096, 11008], P('branch', 'fsdp'), may hold values from -0.09375 to 0.09375
- down_weight: bfloat16 [4, 4096, 11008], P('branch', 'fsdp'), may hold values from -0.0546875 to 0.0546875
Outputs:
- merged_attention: bfloat16 [4096, 4096], P('fsdp', 'branch')
- mixed_out: bfloat16 [1024, 4096], P('fsdp', 'branch')
- token_grads: bfloat16 [1024, 4096], P('fsdp', 'branch')
- gate_grads: bfloat16 [4, 4096, 11008], P('branch', None, 'fsdp')
- up_grads: bfloat16 [4, 4096, 11008], P('branch', None, 'fsdp')
- down_grads: bfloat16 [4, 4096, 11008], P('branch', None, 'fsdp')
Inputs may be any that keep to these rules, and one draw needn't show every extreme that they name: `route_ids`: each row names two different experts; within each aligned block of 32 rows no expert is named by more than 18 rows, a bound that some block reaches.
All inputs are finite; a program needn't handle non-finite values.
Results may differ from a plain program's by a relative error of at most 0.013.
Values may be sent and summed in bfloat16 or wider, within the bound.
No kernel may reach another device: no remote copies, remote signals or barrier semaphores. Data moves between devices by JAX's collectives and lax.ppermute only.
A program may use at most 192 MiB of HBM per device.

v0:
```python
import jax
import jax.numpy as jnp
from jax import lax
from jax.sharding import PartitionSpec as P

CAP = 18


def slot_tables(route_ids, route_gates, experts, capacity):
    expert_ids = lax.broadcasted_iota(jnp.int32, (experts, 1, 1), 0)
    matched = route_ids[None, :, :] == expert_ids
    chosen = jnp.any(matched, axis=2).astype(jnp.int32)
    token_gate = jnp.sum(jnp.where(matched, route_gates[None, :, :], jnp.float32(0.0)), axis=2)
    position = jnp.cumsum(chosen, axis=1) - chosen
    slot_ids = lax.broadcasted_iota(jnp.int32, (1, capacity, 1), 1)
    selector = ((position[:, None, :] == slot_ids) & (chosen[:, None, :] == 1)).astype(jnp.float32)
    slot_gate = jnp.sum(selector * token_gate[:, None, :], axis=2)
    return (selector, slot_gate)


def slot_rows(shard, weights, expert):
    highest = lax.Precision.HIGHEST
    whole = lax.all_gather(shard, "branch", axis=1, tiled=True)
    mine = lax.dynamic_index_in_dim(weights, expert, 0, keepdims=False)
    picked = jnp.dot(mine, whole.astype(jnp.float32), precision=highest)
    return picked.astype(jnp.bfloat16)


def on_device(
    attention_out, tokens, out_grads, route_ids, route_gates, gate_weight, up_weight, down_weight
):
    highest = lax.Precision.HIGHEST
    contract_last = (((1,), (1,)), ((), ()))
    contract_first = (((0,), (0,)), ((), ()))
    branches = lax.axis_size("branch")
    expert = lax.axis_index("branch")
    local_attention = attention_out[0].astype(jnp.float32)
    summed = lax.psum(local_attention.astype(jnp.bfloat16), "branch").astype(jnp.float32)
    share_width = summed.shape[1] // branches
    mine = lax.dynamic_slice_in_dim(summed, expert * share_width, share_width, 1)
    merged_attention = (mine / branches).astype(jnp.bfloat16)
    gate_cols, up_cols, down_cols = (
        lax.all_to_all(gate_weight, "fsdp", split_axis=2, concat_axis=1, tiled=True),
        lax.all_to_all(up_weight, "fsdp", split_axis=2, concat_axis=1, tiled=True),
        lax.all_to_all(down_weight, "fsdp", split_axis=2, concat_axis=1, tiled=True),
    )
    gate_cols, up_cols, down_cols = (gate_cols[0], up_cols[0], down_cols[0])
    selector, slot_gate = slot_tables(route_ids, route_gates, branches, CAP)
    weighted = selector * slot_gate[:, :, None]
    my_select = lax.dynamic_index_in_dim(selector, expert, 0, keepdims=False)
    my_weighted = lax.dynamic_index_in_dim(weighted, expert, 0, keepdims=False)
    slot_inputs = slot_rows(tokens, selector, expert)
    rows_in = lax.all_gather(slot_inputs, "fsdp", axis=0, tiled=True)
    gate_pre = jnp.dot(rows_in, gate_cols, preferred_element_type=jnp.float32)
    up_pre = jnp.dot(rows_in, up_cols, preferred_element_type=jnp.float32)
    sigmoid = jax.nn.sigmoid(gate_pre)
    activated = gate_pre * sigmoid
    hidden = (activated * up_pre).astype(jnp.bfloat16)
    expert_out = lax.psum_scatter(
        lax.dot_general(hidden, down_cols, contract_last, preferred_element_type=jnp.float32),
        "fsdp",
        scatter_dimension=0,
        tiled=True,
    )
    spread = lax.dot_general(my_weighted, expert_out, contract_first, precision=highest)
    mixed = lax.psum_scatter(spread, "branch", scatter_dimension=1, tiled=True)
    mixed_out = mixed.astype(jnp.bfloat16)
    slot_grads = slot_rows(out_grads, weighted, expert)
    rows_grad = lax.all_gather(slot_grads, "fsdp", axis=0, tiled=True)
    hidden_grad = jnp.dot(rows_grad, down_cols, preferred_element_type=jnp.float32)
    down_grads = lax.dot_general(
        rows_grad, hidden, contract_first, preferred_element_type=jnp.float32
    ).astype(jnp.bfloat16)
    gate_delta = (hidden_grad * up_pre * sigmoid * (1.0 + gate_pre * (1.0 - sigmoid))).astype(
        jnp.bfloat16
    )
    up_delta = (hidden_grad * activated).astype(jnp.bfloat16)
    gate_grads = lax.dot_general(
        rows_in, gate_delta, contract_first, preferred_element_type=jnp.float32
    ).astype(jnp.bfloat16)
    up_grads = lax.dot_general(
        rows_in, up_delta, contract_first, preferred_element_type=jnp.float32
    ).astype(jnp.bfloat16)
    total = lax.dot_general(
        gate_delta, gate_cols, contract_last, preferred_element_type=jnp.float32
    )
    input_grad = lax.psum_scatter(
        total
        + lax.dot_general(up_delta, up_cols, contract_last, preferred_element_type=jnp.float32),
        "fsdp",
        scatter_dimension=0,
        tiled=True,
    )
    spread_back = lax.dot_general(my_select, input_grad, contract_first, precision=highest)
    token_grads = lax.psum_scatter(spread_back, "branch", scatter_dimension=1, tiled=True).astype(
        jnp.bfloat16
    )
    return (
        merged_attention,
        mixed_out,
        token_grads,
        gate_grads[None],
        up_grads[None],
        down_grads[None],
    )


def solution(mesh):
    return jax.shard_map(
        on_device,
        mesh=mesh,
        in_specs=(
            P("branch", "fsdp", None),
            P("fsdp", "branch"),
            P("fsdp", "branch"),
            P("fsdp", None),
            P("fsdp", None),
            P("branch", "fsdp", None),
            P("branch", "fsdp", None),
            P("branch", "fsdp", None),
        ),
        out_specs=(
            P("fsdp", "branch"),
            P("fsdp", "branch"),
            P("fsdp", "branch"),
            P("branch", None, "fsdp"),
            P("branch", None, "fsdp"),
            P("branch", None, "fsdp"),
        ),
        check_vma=False,
    )
```

profile of v0, /device:TPU:1, one launch (start us, length us, event | category | flops | bytes accessed | tf_op | source)
XLA Modules:
  0.0 932.2 jit_solution(12510940441068390739)
XLA Ops:
  9.0 8.8 all_gather.12
  18.8 7.6 all_gather.14
  28.2 12.4 %copy.40 = bf16[1,128,11008]{1,0,2:T(2,128)(2,1)} copy(bf16[1,128,11008]{2,1,0:T(8,128)(2,1)} %param.13) | data formatting | bytes 5636096 | tf_op args[5]
  41.2 60.2 %reduce = bf16[11008,128]{1,0:T(8,128)(2,1)S(1)} reduce(bf16[11008,1,128]{2,1,0:T(2,128)(2,1)} %bitcast.85, bf16[]{:T(256)} %broadcast.35), dimensions={1}, to_apply=%bitcast.64.reduce_sub_computation | reduce | bytes 5636098
  103.7 9.3 %all-to-all-start = ((bf16[32,2,22016]{2,1,0:T(2,128)(2,1)}), bf16[32,2,22016]{2,1,0:T(2,128)(2,1)S(1)}, u32[]{:S(2)}, u32[]{:S(2)}) async-start(bf16[32,2,22016]{2,1,0:T(2,128)(2,1)} %reshape.43), calls=%async_computation | async-start | bytes 5636096 | tf_op jit(solution)/shard_map/all_to_all | solution.py:43
  113.0 12.4 %copy.42 = bf16[1,128,11008]{1,0,2:T(2,128)(2,1)} copy(bf16[1,128,11008]{2,1,0:T(8,128)(2,1)} %param.14) | data formatting | bytes 5636096 | tf_op args[6]
  125.4 61.8 %reduce.1 = bf16[11008,128]{1,0:T(8,128)(2,1)} reduce(bf16[11008,1,128]{2,1,0:T(2,128)(2,1)} %bitcast.90, bf16[]{:T(256)} %broadcast.35), dimensions={1}, to_apply=%bitcast.62.reduce_sub_computation | reduce | bytes 5636098
  187.2 7.2 reshape.41
  194.4 8.5 all-to-all-start.1
  202.9 12.4 %copy.44 = bf16[1,128,11008]{1,0,2:T(2,128)(2,1)} copy(bf16[1,128,11008]{2,1,0:T(8,128)(2,1)} %param.15) | data formatting | bytes 5636096 | tf_op args[7]
  215.3 61.8 %reduce.2 = bf16[11008,128]{1,0:T(8,128)(2,1)} reduce(bf16[11008,1,128]{2,1,0:T(2,128)(2,1)} %bitcast.86, bf16[]{:T(256)} %broadcast.35), dimensions={1}, to_apply=%bitcast.66.reduce_sub_computation | reduce | bytes 5636098
  277.1 7.2 reshape.45
  284.3 8.0 all-to-all-start.2
  293.1 11.9 %reshape.44 = bf16[11008,1,128]{2,1,0:T(2,128)(2,1)} reshape(bf16[32,2,22016]{2,1,0:T(2,128)(2,1)S(1)} %all-to-all-done) | data formatting | bytes 5636096
  309.1 18.4 %reshape.42 = bf16[11008,1,128]{2,1,0:T(2,128)(2,1)} reshape(bf16[32,2,22016]{2,1,0:T(2,128)(2,1)} %all-to-all-done.1) | data formatting | bytes 5636096
  333.0 16.9 %all-to-all-done.2 = bf16[32,2,22016]{2,1,0:T(2,128)(2,1)} async-done(((bf16[32,2,22016]{2,1,0:T(2,128)(2,1)}), bf16[32,2,22016]{2,1,0:T(2,128)(2,1)}, u32[]{:S(2)}, u32[]{:S(2)}) %all-to-all-start.2) | async-done | bytes 2818080 | tf_op jit(solution)/shard_map/all_to_all | solution.py:45
  349.9 18.4 %reshape.46 = bf16[11008,1,128]{2,1,0:T(2,128)(2,1)} reshape(bf16[32,2,22016]{2,1,0:T(2,128)(2,1)} %all-to-all-done.2) | data formatting | bytes 5636096
  373.7 7.7 reshape.36
  391.3 7.9 reshape.38
  415.2 6.7 convolution_add_fusion
  421.9 266.7 %fusion.45 = (f32[24,4096]{1,0:T(8,128)S(1)}, f32[24,4096]{1,0:T(8,128)}) fusion(f32[576,4096]{1,0:T(8,128)} %fusion.9, f32[576,4096]{1,0:T(8,128)} %convolution_add_fusion), kind=kCustom, calls=%all-reduce-scatter.2 | all-reduce-scatter fusion | flops 6291457 | bytes 19661312
  703.6 12.0 %collective-permute-done.7 = f32[18,4096]{1,0:T(8,128)S(1)} collective-permute-done((f32[18,4096]{1,0:T(8,128)S(1)}, f32[18,4096]{1,0:T(8,128)S(1)}, u32[]{:S(2)}, u32[]{:S(2)}) %collective-permute-start.7) | collective-permute-done | bytes 294944
  715.5 7.1 collective-permute-start.2
  729.2 19.8 %collective-permute-done.3 = f32[24,4096]{1,0:T(8,128)S(1)} collective-permute-done((f32[24,4096]{1,0:T(8,128)S(1)}, f32[24,4096]{1,0:T(8,128)S(1)}, u32[]{:S(2)}, u32[]{:S(2)}) %collective-permute-start.3) | collective-permute-done | bytes 393248
  750.5 18.1 %concatenate = f32[210,4096]{1,0:T(8,128)S(1)} concatenate(f32[18,4096]{1,0:T(8,128)} %copy-done.13, f32[24,4096]{1,0:T(8,128)} %copy-done.11, f32[24,4096]{1,0:T(8,128)} %copy-done.12, f32[24,4096]{1,0:T(8,128)} %copy-done.14, f32[24,4096]{1,0:T(8,128)} %copy-done.15, f32[24,4096]{1,0:T(8,128)} %copy-done.17, f32[24,4096]{1,0:T(8,128)} %copy-done.18, ...), dimensions={0} | concatenate | bytes 6881280
  771.6 9.9 %collective-permute-start.13 = (f32[24,4096]{1,0:T(8,128)}, f32[24,4096]{1,0:T(8,128)S(1)}, u32[]{:S(2)}, u32[]{:S(2)}) collective-permute-start(f32[24,4096]{1,0:T(8,128)} %get-tuple-element.9), channel_id=1, source_target_pairs={{0,6},{1,7},{2,8},{3,9},{4,10},{5,11},{6,12},{7,13},{8,14},{9,15},... | collective-permute-start | bytes 1179656
  782.6 9.5 %collective-permute-start.15 = (f32[18,4096]{1,0:T(8,128)S(1)}, f32[18,4096]{1,0:T(8,128)S(1)}, u32[]{:S(2)}, u32[]{:S(2)}) collective-permute-start(f32[18,4096]{1,0:T(8,128)S(1)} %slice.1), channel_id=1, source_target_pairs={{0,8},{1,9},{2,10},{3,11},{4,12},{5,13},{6,14},{7,15},{8,16},{9,17... | collective-permute-start | bytes 884744
  794.5 10.1 %collective-permute-start.11 = (f32[24,4096]{1,0:T(8,128)}, f32[24,4096]{1,0:T(8,128)S(1)}, u32[]{:S(2)}, u32[]{:S(2)}) collective-permute-start(f32[24,4096]{1,0:T(8,128)} %get-tuple-element.9), channel_id=1, source_target_pairs={{0,4},{1,5},{2,6},{3,7},{4,8},{5,9},{6,10},{7,11},{8,12},{9,13},{1... | collective-permute-start | bytes 1179656
  804.7 22.1 %collective-permute-start.10 = (f32[24,4096]{1,0:T(8,128)}, f32[24,4096]{1,0:T(8,128)S(1)}, u32[]{:S(2)}, u32[]{:S(2)}) collective-permute-start(f32[24,4096]{1,0:T(8,128)} %get-tuple-element.9), channel_id=1, source_target_pairs={{0,3},{1,4},{2,5},{3,6},{4,7},{5,8},{6,9},{7,10},{8,11},{9,12},{10... | collective-permute-start | bytes 1179656
  828.1 12.1 %collective-permute-start.8 = (f32[24,4096]{1,0:T(8,128)}, f32[24,4096]{1,0:T(8,128)}, u32[]{:S(2)}, u32[]{:S(2)}) collective-permute-start(f32[24,4096]{1,0:T(8,128)} %get-tuple-element.9), channel_id=1, source_target_pairs={{0,1},{1,2},{2,3},{3,4},{4,5},{5,6},{6,7},{7,8},{8,9},{9,10},{10,1... | collective-permute-start | bytes 1179656
  847.7 26.3 %concatenate.1 = f32[210,4096]{1,0:T(8,128)} concatenate(f32[18,4096]{1,0:T(8,128)S(1)} %collective-permute-done.15, f32[24,4096]{1,0:T(8,128)S(1)} %collective-permute-done.14, f32[24,4096]{1,0:T(8,128)S(1)} %collective-permute-done.13, f32[24,4096]{1,0:T(8,128)S(1)} %collective-permute-done.12, f32[24,4096]{1,0:T(8,128)S(1)} %collective-permute-done.11, ...), dimensions={0} | concatenate | bytes 6881280
  892.2 30.5 %reduce-scatter.9.cloned.1.call-done = f32[32,1024]{1,0:T(8,128)} async-done(((f32[32,4096]{1,0:T(8,128)}), f32[32,1024]{1,0:T(8,128)}) %reduce-scatter.9.cloned.1.call-update) | async-done | bytes 131088 | tf_op jit(solution)/shard_map/reduce_scatter | solution.py:95
  (119 shorter events, 105.1 us)
Async XLA Ops:
  8.0 365.7 %all-gather.5.cloned.1.call-start = ((), (), s32[]{:S(2)}) async-start(), calls=%async_computation.8 | async-start | bytes 6488064 | tf_op jit(solution)/shard_map/all_gather | solution.py:53
  18.7 372.6 %all-gather.7.cloned.1.call-start = ((), (), s32[]{:S(2)}) async-start(), calls=%async_computation.9 | async-start | bytes 6488064 | tf_op jit(solution)/shard_map/all_gather | solution.py:69
  103.7 90.7 %all-to-all-start = ((bf16[32,2,22016]{2,1,0:T(2,128)(2,1)}), bf16[32,2,22016]{2,1,0:T(2,128)(2,1)S(1)}, u32[]{:S(2)}, u32[]{:S(2)}) async-start(bf16[32,2,22016]{2,1,0:T(2,128)(2,1)} %reshape.43), calls=%async_computation | async-start | bytes 5636096 | tf_op jit(solution)/shard_map/all_to_all | solution.py:43
  194.4 89.9 %all-to-all-start.1 = ((bf16[32,2,22016]{2,1,0:T(2,128)(2,1)}), bf16[32,2,22016]{2,1,0:T(2,128)(2,1)}, u32[]{:S(2)}, u32[]{:S(2)}) async-start(bf16[32,2,22016]{2,1,0:T(2,128)(2,1)} %reshape.41), calls=%async_computation.1 | async-start | bytes 5636096 | tf_op jit(solution)/shard_map/all_to_all | solution.py:44
  284.3 65.6 %all-to-all-start.2 = ((bf16[32,2,22016]{2,1,0:T(2,128)(2,1)}), bf16[32,2,22016]{2,1,0:T(2,128)(2,1)}, u32[]{:S(2)}, u32[]{:S(2)}) async-start(bf16[32,2,22016]{2,1,0:T(2,128)(2,1)} %reshape.45), calls=%async_computation.2 | async-start | bytes 5636096 | tf_op jit(solution)/shard_map/all_to_all | solution.py:45
  292.3 548.0 %all-reduce.7.cloned.1.call-start = ((), (), s32[]{:S(2)}) async-start(), calls=%async_computation.5 | async-start | bytes 2097152 | tf_op jit(solution)/shard_map/psum | solution.py:38
  292.9 597.7 %reduce-scatter.7.cloned.1.call-start = ((), (), s32[]{:S(2)}) async-start(), calls=%async_computation.6 | async-start | bytes 655360 | tf_op jit(solution)/shard_map/reduce_scatter | solution.py:66
  405.9 9.3 %copy-start.5 = (bf16[576,344]{0,1:T(8,128)(2,1)}, bf16[576,344]{0,1:T(8,128)(2,1)S(1)}, u32[]{:S(2)}) copy-start(bf16[576,344]{0,1:T(8,128)(2,1)S(1)} %get-tuple-element.10) | copy-start | bytes 1188868
  408.6 6.6 copy-start.1
  421.9 306.0 %copy-start.19 = (u32[128]{0:T(128)S(1)}, u32[128]{0:T(128)}, u32[]{:S(2)}) copy-start(u32[128]{0:T(128)} %constant.45) | copy-start | bytes 1540
  688.6 60.3 %copy-start.4 = (f32[24,4096]{1,0:T(8,128)}, f32[24,4096]{1,0:T(8,128)S(1)}, u32[]{:S(2)}) copy-start(f32[24,4096]{1,0:T(8,128)S(1)} %get-tuple-element.8) | copy-start | bytes 1179652
  688.6 34.0 %collective-permute-start.6 = (f32[24,4096]{1,0:T(8,128)S(1)}, f32[24,4096]{1,0:T(8,128)S(1)}, u32[]{:S(2)}, u32[]{:S(2)}) collective-permute-start(f32[24,4096]{1,0:T(8,128)S(1)} %get-tuple-element.8), channel_id=1, source_target_pairs={{0,7},{1,8},{2,9},{3,10},{4,11},{5,12},{6,13},{7,14},{8,15},{9,16}... | collective-permute-start | bytes 1179656
  689.9 34.3 %collective-permute-start.5 = (f32[24,4096]{1,0:T(8,128)S(1)}, f32[24,4096]{1,0:T(8,128)S(1)}, u32[]{:S(2)}, u32[]{:S(2)}) collective-permute-start(f32[24,4096]{1,0:T(8,128)S(1)} %get-tuple-element.8), channel_id=1, source_target_pairs={{0,6},{1,7},{2,8},{3,9},{4,10},{5,11},{6,12},{7,13},{8,14},{9,15},... | collective-permute-start | bytes 1179656
  691.3 24.2 %collective-permute-start.7 = (f32[18,4096]{1,0:T(8,128)S(1)}, f32[18,4096]{1,0:T(8,128)S(1)}, u32[]{:S(2)}, u32[]{:S(2)}) collective-permute-start(f32[18,4096]{1,0:T(8,128)S(1)} %slice), channel_id=1, source_target_pairs={{0,8},{1,9},{2,10},{3,11},{4,12},{5,13},{6,14},{7,15},{8,16},{9,17... | collective-permute-start | bytes 884744
  695.7 33.4 %collective-permute-start.4 = (f32[24,4096]{1,0:T(8,128)S(1)}, f32[24,4096]{1,0:T(8,128)S(1)}, u32[]{:S(2)}, u32[]{:S(2)}) collective-permute-start(f32[24,4096]{1,0:T(8,128)S(1)} %get-tuple-element.8), channel_id=1, source_target_pairs={{0,5},{1,6},{2,7},{3,8},{4,9},{5,10},{6,11},{7,12},{8,13},{9,14},{... | collective-permute-start | bytes 1179656
  698.8 50.1 %collective-permute-start.3 = (f32[24,4096]{1,0:T(8,128)S(1)}, f32[24,4096]{1,0:T(8,128)S(1)}, u32[]{:S(2)}, u32[]{:S(2)}) collective-permute-start(f32[24,4096]{1,0:T(8,128)S(1)} %get-tuple-element.8), channel_id=1, source_target_pairs={{0,4},{1,5},{2,6},{3,7},{4,8},{5,9},{6,10},{7,11},{8,12},{9,13},{1... | collective-permute-start | bytes 1179656
  715.5 12.4 %copy-start.13 = (f32[18,4096]{1,0:T(8,128)}, f32[18,4096]{1,0:T(8,128)S(1)}, u32[]{:S(2)}) copy-start(f32[18,4096]{1,0:T(8,128)S(1)} %collective-permute-done.7) | copy-start | bytes 884740
  715.5 33.4 %collective-permute-start.2 = (f32[24,4096]{1,0:T(8,128)S(1)}, f32[24,4096]{1,0:T(8,128)S(1)}, u32[]{:S(2)}, u32[]{:S(2)}) collective-permute-start(f32[24,4096]{1,0:T(8,128)S(1)} %get-tuple-element.8), channel_id=1, source_target_pairs={{0,3},{1,4},{2,5},{3,6},{4,7},{5,8},{6,9},{7,10},{8,11},{9,12},{10... | collective-permute-start | bytes 1179656
  722.7 26.2 %collective-permute-start.1 = (f32[24,4096]{1,0:T(8,128)S(1)}, f32[24,4096]{1,0:T(8,128)S(1)}, u32[]{:S(2)}, u32[]{:S(2)}) collective-permute-start(f32[24,4096]{1,0:T(8,128)S(1)} %get-tuple-element.8), channel_id=1, source_target_pairs={{0,2},{1,3},{2,4},{3,5},{4,6},{5,7},{6,8},{7,9},{8,10},{9,11},{10,... | collective-permute-start | bytes 1179656
  724.3 26.3 %collective-permute-start = (f32[24,4096]{1,0:T(8,128)S(1)}, f32[24,4096]{1,0:T(8,128)}, u32[]{:S(2)}, u32[]{:S(2)}) collective-permute-start(f32[24,4096]{1,0:T(8,128)S(1)} %get-tuple-element.8), channel_id=1, source_target_pairs={{0,1},{1,2},{2,3},{3,4},{4,5},{5,6},{6,7},{7,8},{8,9},{9,10},{10,1... | collective-permute-start | bytes 1179656
  729.1 19.8 %copy-start.14 = (f32[24,4096]{1,0:T(8,128)}, f32[24,4096]{1,0:T(8,128)S(1)}, u32[]{:S(2)}) copy-start(f32[24,4096]{1,0:T(8,128)S(1)} %collective-permute-done.4) | copy-start | bytes 1179652
  770.2 152.5 %reduce-scatter.9.cloned.1.call-start = ((), (), s32[]{:S(2)}) async-start(), calls=%async_computation.7 | async-start | bytes 655360 | tf_op jit(solution)/shard_map/reduce_scatter | solution.py:95
  770.3 56.6 %collective-permute-start.14 = (f32[24,4096]{1,0:T(8,128)}, f32[24,4096]{1,0:T(8,128)S(1)}, u32[]{:S(2)}, u32[]{:S(2)}) collective-permute-start(f32[24,4096]{1,0:T(8,128)} %get-tuple-element.9), channel_id=1, source_target_pairs={{0,7},{1,8},{2,9},{3,10},{4,11},{5,12},{6,13},{7,14},{8,15},{9,16}... | collective-permute-start | bytes 1179656
  771.6 56.6 %collective-permute-start.13 = (f32[24,4096]{1,0:T(8,128)}, f32[24,4096]{1,0:T(8,128)S(1)}, u32[]{:S(2)}, u32[]{:S(2)}) collective-permute-start(f32[24,4096]{1,0:T(8,128)} %get-tuple-element.9), channel_id=1, source_target_pairs={{0,6},{1,7},{2,8},{3,9},{4,10},{5,11},{6,12},{7,13},{8,14},{9,15},... | collective-permute-start | bytes 1179656
  782.6 22.1 %collective-permute-start.15 = (f32[18,4096]{1,0:T(8,128)S(1)}, f32[18,4096]{1,0:T(8,128)S(1)}, u32[]{:S(2)}, u32[]{:S(2)}) collective-permute-start(f32[18,4096]{1,0:T(8,128)S(1)} %slice.1), channel_id=1, source_target_pairs={{0,8},{1,9},{2,10},{3,11},{4,12},{5,13},{6,14},{7,15},{8,16},{9,17... | collective-permute-start | bytes 884744
  792.0 50.0 %collective-permute-start.12 = (f32[24,4096]{1,0:T(8,128)}, f32[24,4096]{1,0:T(8,128)S(1)}, u32[]{:S(2)}, u32[]{:S(2)}) collective-permute-start(f32[24,4096]{1,0:T(8,128)} %get-tuple-element.9), channel_id=1, source_target_pairs={{0,5},{1,6},{2,7},{3,8},{4,9},{5,10},{6,11},{7,12},{8,13},{9,14},{... | collective-permute-start | bytes 1179656
  794.5 47.4 %collective-permute-start.11 = (f32[24,4096]{1,0:T(8,128)}, f32[24,4096]{1,0:T(8,128)S(1)}, u32[]{:S(2)}, u32[]{:S(2)}) collective-permute-start(f32[24,4096]{1,0:T(8,128)} %get-tuple-element.9), channel_id=1, source_target_pairs={{0,4},{1,5},{2,6},{3,7},{4,8},{5,9},{6,10},{7,11},{8,12},{9,13},{1... | collective-permute-start | bytes 1179656
  804.7 37.3 %collective-permute-start.10 = (f32[24,4096]{1,0:T(8,128)}, f32[24,4096]{1,0:T(8,128)S(1)}, u32[]{:S(2)}, u32[]{:S(2)}) collective-permute-start(f32[24,4096]{1,0:T(8,128)} %get-tuple-element.9), channel_id=1, source_target_pairs={{0,3},{1,4},{2,5},{3,6},{4,7},{5,8},{6,9},{7,10},{8,11},{9,12},{10... | collective-permute-start | bytes 1179656
  826.8 15.2 %collective-permute-start.9 = (f32[24,4096]{1,0:T(8,128)}, f32[24,4096]{1,0:T(8,128)S(1)}, u32[]{:S(2)}, u32[]{:S(2)}) collective-permute-start(f32[24,4096]{1,0:T(8,128)} %get-tuple-element.9), channel_id=1, source_target_pairs={{0,2},{1,3},{2,4},{3,5},{4,6},{5,7},{6,8},{7,9},{8,10},{9,11},{10,... | collective-permute-start | bytes 1179656
  828.1 19.5 %collective-permute-start.8 = (f32[24,4096]{1,0:T(8,128)}, f32[24,4096]{1,0:T(8,128)}, u32[]{:S(2)}, u32[]{:S(2)}) collective-permute-start(f32[24,4096]{1,0:T(8,128)} %get-tuple-element.9), channel_id=1, source_target_pairs={{0,1},{1,2},{2,3},{3,4},{4,5},{5,6},{6,7},{7,8},{8,9},{9,10},{10,1... | collective-permute-start | bytes 1179656
  842.0 34.3 %copy-start.10 = (bf16[576,344]{0,1:T(8,128)(2,1)S(1)}, bf16[576,344]{0,1:T(8,128)(2,1)}, u32[]{:S(2)}) copy-start(bf16[576,344]{0,1:T(8,128)(2,1)} %copy-done.9) | copy-start | bytes 1188868
  847.7 35.0 %slice-start = ((s8[4718592]{0:T(1024)(128)(4,1)}), s8[524288]{0:T(1024)(128)(4,1)S(1)}, s32[]{:S(2)}) async-start(s8[4718592]{0:T(1024)(128)(4,1)} %bitcast.100), calls=%async_computation.10 | async-start | bytes 1048576
  (14 other events, 45.8 us)
Sparse Core Ops, SparseCore 0:
  18.8 169.3 all-gather.4
  190.0 200.2 all-gather.6
Sparse Core Ops, SparseCore 1:
  295.3 69.9 all-reduce.6
  770.3 49.9 reduce-scatter.6
  876.4 46.2 reduce-scatter.8
where the time goes:
time: 944 us; the launch traced here: 932 us
  blocking collectives  283 us (30%)
  other arithmetic  190 us (20%)
  local copies, waits for them, and re-layouts  182 us (19%)
  starting transfers between devices  122 us (13%)
  waiting for transfers between devices  84.7 us (9%)
  matrix products  52.4 us (6%)
  between operations  17.2 us (2%)
    unnamed x1, blocking collectives  267 us
    unnamed x4, other arithmetic  184 us
    unnamed x64, local copies, waits for them, and re-layouts  178 us
    unnamed x16, starting transfers between devices  96 us
    unnamed x21, waiting for transfers between devices  37.3 us
    reduce_scatter x1, waiting for transfers between devices, on_device(): lax.psum_scatter(spread_back, 'branch', scatter_dimension=1, tiled=True)  30.5 us
  transfers between devices with their start and end apart: 24, of which 5 were waited for; matrix products, arithmetic and copies ran while one was open for 74% of the time, Pallas kernels for 0%

commit v1 on v0

v1 whole, which is shorter than its diff:
```python
import jax
import jax.numpy as jnp
from jax import lax
from jax.experimental import pallas as pl
from jax.experimental.pallas import tpu as pltpu
from jax.sharding import Mesh
from jax.sharding import PartitionSpec as P

CAP = 18
BLK = 32
GROUPS = 4
BF = jnp.bfloat16
F32 = jnp.float32
BRANCH = ("xh", "c")
FSDP = ("xl", "z", "y")
PLANE = ("xh", "xl", "z", "y")
CONTRACT_LAST = (((1,), (1,)), ((), ()))
CONTRACT_FIRST = (((0,), (0,)), ((), ()))
VMEM = 44 * 2**20


def call(kernel, prefetch, grid, ins, outs, shapes, name, scratch=()):
    return pl.pallas_call(
        kernel,
        grid_spec=pltpu.PrefetchScalarGridSpec(
            num_scalar_prefetch=prefetch,
            grid=grid,
            in_specs=ins,
            out_specs=outs,
            scratch_shapes=scratch,
        ),
        out_shape=shapes,
        compiler_params=pltpu.CompilerParams(vmem_limit_bytes=VMEM),
        cost_estimate=pl.CostEstimate(flops=1, bytes_accessed=1, transcendentals=0),
        name=name,
    )


def transpose_kernel(w_ref, o_ref):
    o_ref[...] = w_ref[0].T


def transposed(w):
    depth, width = w.shape[1:]
    step = width // 2
    blocks = call(
        transpose_kernel,
        0,
        (2,),
        [pl.BlockSpec((1, depth, step), lambda i: (0, 0, i))],
        pl.BlockSpec((step, depth), lambda i: (i, 0)),
        jax.ShapeDtypeStruct((width, depth), BF),
        "transpose_weight",
    )(w)
    return blocks.reshape(BLK, width // BLK, depth)


def to_owners(blocks):
    return lax.all_to_all(blocks, FSDP, 0, 0, tiled=True)


def wide(ref, first, count):
    return jnp.concatenate([ref[first + j] for j in range(count)], axis=1)


def pick_kernel(sel_ref, gate_ref, x_ref, o_ref):
    factor = jnp.where(pl.program_id(1) == 1, gate_ref[...], F32(1.0))
    slots = sel_ref.shape[1]
    for g in range(GROUPS):
        at = pl.ds(g * slots, slots)
        rows = jnp.dot(sel_ref[g], x_ref[0, g], preferred_element_type=F32)
        o_ref[0, 0, at, :] = (rows * factor[g * slots : (g + 1) * slots]).astype(BF)


def picked_rows(selector, slot_gate, gathered):
    _, slots, per = selector.shape
    width = gathered.shape[3] // 128 // 2 * 128
    total = GROUPS * slots
    return call(
        pick_kernel,
        0,
        (2, 2),
        [
            pl.BlockSpec((GROUPS, slots, per), lambda x, k: (0, 0, 0)),
            pl.BlockSpec((total, 1), lambda x, k: (0, 0)),
            pl.BlockSpec((1, GROUPS, per, width), lambda x, k: (x, 0, 0, k)),
        ],
        pl.BlockSpec((1, 1, total, width), lambda x, k: (k, x, 0, 0)),
        jax.ShapeDtypeStruct((2, 2, total, width), BF),
        "pick_rows",
    )(selector, slot_gate, gathered)


def spread_tokens(spread_ref, values, o_ref):
    slots, per = spread_ref.shape[2], spread_ref.shape[1]
    for g in range(GROUPS):
        part = values[g * slots : (g + 1) * slots]
        rows = jnp.dot(spread_ref[g], part, preferred_element_type=F32)
        o_ref[pl.ds(g * per, per), :] = rows.astype(BF)


def accumulate(half, first, mine_ref, theirs_ref, weight_ref, acc_ref):
    cols = wide(weight_ref, 0, weight_ref.shape[0])
    rows = jnp.where(half == 0, mine_ref[0, 0], theirs_ref[0, 0])
    part = lax.dot_general(rows, cols, CONTRACT_LAST, preferred_element_type=F32)

    @pl.when(first)
    def _():
        acc_ref[...] = part

    @pl.when(jnp.logical_not(first))
    def _():
        acc_ref[...] += part


def expert_kernel(
    core_ref, mine_in, theirs_in, mine_grad, theirs_grad, gate_cols, up_cols, down_cols,
    slot_gate, spread, hidden, gate_delta, up_delta, tokens, gate_acc, up_acc, grad_acc,
):
    half, x = pl.program_id(0), pl.program_id(1)
    first = (half == 0) & (x == 0)
    accumulate(half, first, mine_in, theirs_in, gate_cols, gate_acc)
    accumulate(half, first, mine_in, theirs_in, up_cols, up_acc)
    accumulate(half, first, mine_grad, theirs_grad, down_cols, grad_acc)

    @pl.when((half == 1) & (x == 1))
    def _():
        gate_pre, up_pre, hidden_grad = gate_acc[...], up_acc[...], grad_acc[...]
        sigmoid = jax.nn.sigmoid(gate_pre)
        activated = gate_pre * sigmoid
        product = activated * up_pre
        slope = up_pre * sigmoid * (1.0 + gate_pre * (1.0 - sigmoid))
        hidden[...] = product.astype(BF)
        gate_delta[...] = (hidden_grad * slope).astype(BF)
        up_delta[...] = (hidden_grad * activated).astype(BF)
        spread_tokens(spread, (product * slot_gate[...]).astype(BF), tokens.at[0])
        spread_tokens(spread, gate_delta[...], tokens.at[1])
        spread_tokens(spread, up_delta[...], tokens.at[2])


def row_specs(which, total, width):
    return [
        pl.BlockSpec((1, 1, total, width), lambda h, x, c: (which, jnp.where(h == 0, x, 1), 0, 0)),
        pl.BlockSpec((1, 1, total, width), lambda h, x, c: (which, jnp.where(h == 0, 0, x), 0, 0)),
    ]


def whole(shape):
    return pl.BlockSpec(shape, lambda *_: (0,) * len(shape))


def expert(core, mine, theirs, gate_cols, up_cols, down_cols, slot_gate, spread):
    total, width = mine.shape[2:]
    blocks, units, depth = gate_cols.shape
    tokens = spread.shape[0] * spread.shape[1]
    cols = pl.BlockSpec(
        (blocks // 4, units, depth), lambda h, x, c: (2 * x + jnp.where(h == 0, c[0], 1 - c[0]), 0, 0)
    )
    return call(
        expert_kernel,
        1,
        (2, 2),
        row_specs(0, total, width)
        + row_specs(1, total, width)
        + [cols] * 3
        + [whole(slot_gate.shape), whole(spread.shape)],
        [whole((total, units))] * 3 + [whole((3, tokens, units))],
        [jax.ShapeDtypeStruct((total, units), BF)] * 3
        + [jax.ShapeDtypeStruct((3, tokens, units), BF)],
        "expert",
        scratch=[pltpu.VMEM((total, units), F32)] * 3,
    )(core, mine, theirs, mine, theirs, gate_cols, up_cols, down_cols, slot_gate, spread)


def weight_grad_kernel(core_ref, mine, theirs, *refs):
    count = len(refs) // 2
    rows = jnp.where(pl.program_id(0) == 0, mine[0, 0], theirs[0, 0])
    for delta, out in zip(refs[:count], refs[count:]):
        grad = lax.dot_general(rows, delta[...], CONTRACT_FIRST, preferred_element_type=F32)
        out[...] = grad.astype(BF)


def weight_grads(core, mine, theirs, which, deltas):
    total, width = mine.shape[2:]
    units = deltas[0].shape[1]
    rows = row_specs(which, total, width)
    out = pl.BlockSpec(
        (width, units), lambda h, x, c: (2 * x + jnp.where(h == 0, c[0], 1 - c[0]), 0)
    )
    return call(
        weight_grad_kernel,
        1,
        (2, 2),
        rows + [whole(d.shape) for d in deltas],
        [out] * len(deltas),
        [jax.ShapeDtypeStruct((4 * width, units), BF)] * len(deltas),
        "weight_grads",
    )(core, mine, theirs, *deltas)


def partial_kernel(terms, half_ref, *refs):
    o_ref = refs[-1]
    step = 2
    for first in range(0, refs[1].shape[0], step):
        total = None
        for i in range(terms):
            part = jnp.dot(
                refs[2 * i][...], wide(refs[2 * i + 1], first, step), preferred_element_type=F32
            )
            total = part if total is None else total + part
        at = pl.ds(first * refs[1].shape[2], step * refs[1].shape[2])
        o_ref[0, :, at] = total.astype(BF)


def token_partial(terms, half):
    _, tokens, units = terms[0][0].shape
    blocks, _, depth = terms[0][2].shape
    per = blocks // 8
    quarter = 2 * per * depth
    specs, args = [], []
    for rows, i, weight in terms:
        specs.append(pl.BlockSpec((None, tokens, units), lambda x, n, h, i=i: (i, 0, 0)))
        if weight.shape[0] == blocks:
            index = lambda x, n, h: (4 * x + 2 * h[0] + n, 0, 0)
        else:
            index = lambda x, n, h: (2 * x + n, 0, 0)
        specs.append(pl.BlockSpec((per, units, depth), index))
        args += [rows, weight]
    return call(
        lambda *refs: partial_kernel(len(terms), *refs),
        1,
        (2, 2),
        specs,
        pl.BlockSpec((1, tokens, per * depth), lambda x, n, h: (x, 0, n)),
        jax.ShapeDtypeStruct((2, tokens, quarter), BF),
        "token_partial",
    )(half, *args)


def over_core(x):
    return lax.ppermute(x, "c", [(0, 1), (1, 0)])


def half_blocks(cols, half):
    blocks, units, depth = cols.shape
    cut = cols.reshape(2, 2, blocks // 4, units, depth)
    picked = lax.dynamic_index_in_dim(cut, half, 1, keepdims=False)
    return picked.reshape(blocks // 2, units, depth)


def scattered(mine):
    rows, quarter = mine.shape[1] // BLK, mine.shape[2]
    return lax.all_to_all(mine.reshape(2 * BLK, rows, quarter), PLANE, 0, 0, tiled=True)


def summed(parts):
    return jnp.sum(parts.astype(F32), axis=0).astype(BF)


def route_columns(ids, gates):
    columns, rest = [ids.astype(F32)], gates
    for _ in range(3):
        piece = lax.reduce_precision(rest, 8, 7)
        columns.append(piece)
        rest = rest - piece
    columns = jnp.concatenate(columns, axis=1)
    return jnp.pad(columns, ((0, 0), (0, 128 - columns.shape[1]))).astype(BF)


def routes(columns):
    columns = columns.reshape(-1, columns.shape[-1])[:, :8].astype(F32)
    gates = columns[:, 2:4] + columns[:, 4:6] + columns[:, 6:8]
    return columns[:, :2].astype(jnp.int32), gates


def slot_tables(ids, gates, expert):
    matched = ids == expert
    chosen = jnp.any(matched, axis=-1)
    gate = jnp.sum(jnp.where(matched, gates, F32(0.0)), axis=-1)
    counted = chosen.reshape(BLK, -1).astype(jnp.int32)
    position = jnp.cumsum(counted, axis=1) - counted
    per_group = BLK // GROUPS
    slots = per_group * CAP
    base = (lax.broadcasted_iota(jnp.int32, position.shape, 0) % per_group) * CAP
    slot = jnp.where(counted == 1, base + position, -1).reshape(GROUPS, -1)
    shape = (GROUPS, slots, slot.shape[1])
    selector = lax.broadcasted_iota(jnp.int32, shape, 1) == slot[:, None, :]
    slot_gate = jnp.sum(jnp.where(selector, gate.reshape(GROUPS, 1, -1), F32(0.0)), axis=2)
    spread = lax.broadcasted_iota(jnp.int32, (GROUPS, slot.shape[1], slots), 2) == slot[:, :, None]
    return selector.astype(BF), spread.astype(BF), slot_gate.reshape(-1, 1)


def average(attention):
    me = lax.axis_index(BRANCH)
    share = attention.shape[1] // 4

    def quarter(i):
        return lax.dynamic_slice_in_dim(attention, i * share, share, 1)

    total = quarter(me).astype(F32)
    for shift in range(1, 4):
        sent = quarter((me + shift) % 4)
        there = [(i, (i + shift) % 4) for i in range(4)]
        total = total + lax.ppermute(sent, BRANCH, there).astype(F32)
    return (total / 4).astype(BF)


def together(*arrays):
    return lax.optimization_barrier(arrays)


def on_device(
    attention_out, tokens, out_grads, route_ids, route_gates, gate_weight, up_weight, down_weight
):
    core = lax.axis_index("c")
    expert_id = 2 * lax.axis_index("xh") + core
    sibling = 2 * lax.axis_index("xh") + 1 - core
    core_id = core.reshape(1).astype(jnp.int32)

    width = tokens.shape[1]
    both = jnp.concatenate([tokens, out_grads, route_columns(route_ids, route_gates)], axis=1)
    gathered = lax.all_gather(both, PLANE, axis=0, tiled=True)
    gathered = gathered.reshape(2, GROUPS, -1, both.shape[1])

    gate_blocks = transposed(gate_weight)
    up_blocks, down_blocks = transposed(up_weight), transposed(down_weight)
    gate_cols = to_owners(gate_blocks)
    gate_cols, up_blocks, down_blocks = together(gate_cols, up_blocks, down_blocks)
    up_cols = to_owners(up_blocks)
    up_cols, down_blocks = together(up_cols, down_blocks)
    down_cols = to_owners(down_blocks)
    their_gate = over_core(half_blocks(gate_cols, 1 - core))
    their_up = over_core(half_blocks(up_cols, 1 - core))
    down_cols, gathered = together(down_cols, gathered)

    ids, gates = routes(gathered[0, :, :, 2 * width :])
    selector, spread, slot_gate = slot_tables(ids, gates, expert_id)
    other_selector, _, other_gate = slot_tables(ids, gates, sibling)
    theirs = over_core(picked_rows(other_selector, other_gate, gathered))
    their_down = over_core(half_blocks(down_cols, 1 - core))
    mine = picked_rows(selector, slot_gate, gathered)
    attention, mine = together(attention_out[0], mine)
    merged_attention = average(attention)
    hidden, gate_delta, up_delta, by_token = expert(
        core_id, mine, theirs, gate_cols, up_cols, down_cols, slot_gate, spread
    )
    their_token = over_core(by_token)
    total = token_partial([(by_token, 0, down_cols), (their_token, 0, their_down)], core_id)
    total, merged_attention, their_gate, their_up = together(
        total, merged_attention, their_gate, their_up
    )
    out_parts = scattered(total)

    total = token_partial(
        [
            (by_token, 1, gate_cols),
            (by_token, 2, up_cols),
            (their_token, 1, their_gate),
            (their_token, 2, their_up),
        ],
        core_id,
    )
    gate_grads, up_grads = weight_grads(core_id, mine, theirs, 0, [gate_delta, up_delta])
    (down_grads,) = weight_grads(core_id, mine, theirs, 1, [hidden])
    total, gate_grads, up_grads, down_grads = together(total, gate_grads, up_grads, down_grads)
    grad_parts = scattered(total)
    mixed_out = summed(out_parts)
    grad_parts, mixed_out = together(grad_parts, mixed_out)
    token_grads = summed(grad_parts)
    return (
        merged_attention,
        mixed_out,
        token_grads,
        gate_grads[None],
        up_grads[None],
        down_grads[None],
    )


def solution(mesh):
    fine = Mesh(mesh.devices.reshape(2, 2, 2, 4, 4), ("xh", "c", "xl", "z", "y"))
    return jax.shard_map(
        on_device,
        mesh=fine,
        in_specs=(
            P(BRANCH, FSDP, None),
            P(FSDP, BRANCH),
            P(FSDP, BRANCH),
            P(FSDP, None),
            P(FSDP, None),
            P(BRANCH, FSDP, None),
            P(BRANCH, FSDP, None),
            P(BRANCH, FSDP, None),
        ),
        out_specs=(
            P(FSDP, BRANCH),
            P(FSDP, BRANCH),
            P(FSDP, BRANCH),
            P(BRANCH, None, FSDP),
            P(BRANCH, None, FSDP),
            P(BRANCH, None, FSDP),
        ),
        check_vma=False,
    )
```

time: 944 us -> 401 us (0.42)
  blocking collectives: 283 us -> 47.8 us
  other arithmetic: 190 us -> 14.9 us
  local copies, waits for them, and re-layouts: 182 us -> 46.1 us
  waiting for transfers between devices: 84.7 us -> 171 us
  starting transfers between devices: 122 us -> 39.1 us
  Pallas kernels: 0 us -> 64.2 us
  matrix products: 52.4 us -> 0 us
    unnamed x1 -> x0, blocking collectives: 267 us -> none
    unnamed x4 -> x0, other arithmetic: 184 us -> none
    unnamed x64 -> x58, local copies, waits for them, and re-layouts: 178 us -> 31.5 us
    all_to_all x3 -> x4, waiting for transfers between devices: 16.9 us -> 149 us  [the longest x2 82.3 us: to_owners(): return lax.all_to_all(blocks, FSDP, 0, 0, tiled=True)]
    unnamed x16 -> x0, starting transfers between devices: 96 us -> none
    pallas_call x0 -> x10, Pallas kernels: none -> 64.2 us  [the longest x2 19.6 us: token_partial(): call(lambda *refs: partial_kernel(len(terms), *refs), 1, (2, 2), specs, p...]
    dot_general x13 -> x0, matrix products: 52.4 us -> none  [the longest x1 6.72 us: on_device(): lax.dot_general(up_delta, up_cols, contract_last, preferred_element_type=...]
    all_to_all x0 -> x1, blocking collectives: none -> 47.8 us  [to_owners(): return lax.all_to_all(blocks, FSDP, 0, 0, tiled=True)]
  transfers between devices with their start and end apart: 24 -> 13, of which waited for: 5 -> 8; matrix products, arithmetic and copies ran while one was open for 74% -> 7% of each run, Pallas kernels for 0% -> 11%
where the time goes in v1:
time: 401 us; the launch traced here: 397 us
  waiting for transfers between devices  171 us (43%)
  Pallas kernels  64.2 us (16%)
  blocking collectives  47.8 us (12%)
  local copies, waits for them, and re-layouts  46.1 us (11%)
  starting transfers between devices  39.1 us (10%)
  other arithmetic  14.9 us (4%)
  between operations  14.4 us (4%)
    all_to_all x2, waiting for transfers between devices, to_owners(): return lax.all_to_all(blocks, FSDP, 0, 0, tiled=True)  82.3 us
    all_to_all x2, waiting for transfers between devices, scattered(): lax.all_to_all(mine.reshape(2 * BLK, rows, quarter), PLANE, 0, 0, tiled=T...  66.9 us
    all_to_all x1, blocking collectives, to_owners(): return lax.all_to_all(blocks, FSDP, 0, 0, tiled=True)  47.8 us
    unnamed x58, local copies, waits for them, and re-layouts  31.5 us
    pallas_call x2, Pallas kernels, token_partial(): call(lambda *refs: partial_kernel(len(terms), *refs), 1, (2, 2), specs, p...  19.6 us
    ppermute x3, waiting for transfers between devices, average(): total = total + lax.ppermute(sent, BRANCH, there).astype(F32)  17.1 us
    all_to_all x2, starting transfers between devices, scattered(): lax.all_to_all(mine.reshape(2 * BLK, rows, quarter), PLANE, 0, 0, tiled=T...  16.3 us
    all_to_all x2, starting transfers between devices, to_owners(): return lax.all_to_all(blocks, FSDP, 0, 0, tiled=True)  15.8 us
  transfers between devices with their start and end apart: 13, of which 8 were waited for; matrix products, arithmetic and copies ran while one was open for 7% of the time, Pallas kernels for 11%

profile of v1, /device:TPU:1, one launch (start us, length us, event | category | flops | bytes accessed | tf_op | source)
XLA Modules:
  0.0 397.1 jit_solution(5561886311177372479)
XLA Ops:
  14.7 9.8 %all-to-all-start = ((bf16[32,344,128]{2,1,0:T(8,128)(2,1)}), bf16[32,344,128]{2,1,0:T(8,128)(2,1)S(1)}, u32[]{:S(2)}, u32[]{:S(2)}) async-start(bf16[32,344,128]{2,1,0:T(8,128)(2,1)} %bitcast.29), calls=%async_computation | async-start | bytes 5636096 | tf_op jit(solution)/shard_map/all_to_all | solution.py:59
  31.7 28.1 %all-to-all-done.gate_cols.refs_2_ = bf16[32,344,128]{2,1,0:T(8,128)(2,1)S(1)} async-done(((bf16[32,344,128]{2,1,0:T(8,128)(2,1)}), bf16[32,344,128]{2,1,0:T(8,128)(2,1)S(1)}, u32[]{:S(2)}, u32[]{:S(2)}) %all-to-all-start) | async-done | bytes 2818080 | tf_op jit(solution)/shard_map/all_to_all | solution.py:59
  59.8 47.8 %all_to_all.25.up_cols.refs_4_ = bf16[32,344,128]{2,1,0:T(8,128)(2,1)} all-to-all(bf16[32,344,128]{2,1,0:T(8,128)(2,1)} %bitcast.30), channel_id=1, replica_groups=mesh['xh'=2,'c'=2,'xl'=2,'z'=4,'y'=4] {'xl','z','y'}, dimensions={0} | all-to-all | bytes 5636096 | tf_op jit(solution)/shard_map/all_to_all | solution.py:59
  107.5 6.0 %all-to-all-start.2 = ((bf16[32,344,128]{2,1,0:T(8,128)(2,1)}), bf16[32,344,128]{2,1,0:T(8,128)(2,1)S(1)}, u32[]{:S(2)}, u32[]{:S(2)}) async-start(bf16[32,344,128]{2,1,0:T(8,128)(2,1)} %bitcast.28), calls=%async_computation.2 | async-start | bytes 5636096 | tf_op jit(solution)/shard_map/all_to_all | solution.py:59
  113.7 54.2 %all-to-all-done.2.down_cols.refs_2_ = bf16[32,344,128]{2,1,0:T(8,128)(2,1)S(1)} async-done(((bf16[32,344,128]{2,1,0:T(8,128)(2,1)}), bf16[32,344,128]{2,1,0:T(8,128)(2,1)S(1)}, u32[]{:S(2)}, u32[]{:S(2)}) %all-to-all-start.2) | async-done | bytes 2818080 | tf_op jit(solution)/shard_map/all_to_all | solution.py:59
  167.9 4.3 %all-gather.2.cloned.1.call-done = bf16[2048,2176]{1,0:T(8,128)(2,1)} async-done(((bf16[32,2176]{1,0:T(8,128)(2,1)}), bf16[2048,2176]{1,0:T(8,128)(2,1)}) %all-gather.2.cloned.1.call-update) | async-done | bytes 8912912 | tf_op jit(solution)/shard_map/all_gather | solution.py:322
  175.8 6.7 %pick_rows.3 = bf16[2,2,576,1024]{3,2,1,0:T(8,128)(2,1)} custom-call(bf16[4,144,256]{2,1,0:T(8,128)(2,1)S(1)} %fusion.1.sel_ref, f32[576,1]{1,0:T(8,128)S(1)} %reshape.235.gate_ref, bf16[2,4,256,2176]{3,2,1,0:T(8,128)(2,1)} %bitcast.34), custom_call_target="tpu_custom_call" | custom-call | flops 1 | bytes 1 | tf_op jit(solution)/shard_map/pick_rows/pallas_call | solution.py:79
  183.8 5.7 %pick_rows.2.mine_in.mine_grad.mine = bf16[2,2,576,1024]{3,2,1,0:T(8,128)(2,1)S(1)} custom-call(bf16[4,144,256]{2,1,0:T(8,128)(2,1)S(1)} %fusion.2.sel_ref, f32[576,1]{1,0:T(8,128)S(1)} %reshape.234.gate_ref.slot_gate, bf16[2,4,256,2176]{3,2,1,0:T(8,128)(2,1)} %bitcast.35), custom_call_target="tpu_custom_call" | custom-call | flops 1 | bytes 1 | tf_op jit(solution)/shard_map/pick_rows/pallas_call | solution.py:79
  189.5 2.1 copy-done
  191.8 14.6 %expert.1 = (bf16[576,344]{1,0:T(8,128)(2,1)S(1)}, bf16[576,344]{1,0:T(8,128)(2,1)S(1)}, bf16[576,344]{1,0:T(8,128)(2,1)S(1)}, bf16[3,1024,344]{2,1,0:T(8,128)(2,1)S(1)}) custom-call(s32[1]{0:T(128)} %bitcast.core_ref.refs_0_, bf16[2,2,576,1024]{3,2,1,0:T(8,128)(2,1)} %copy-done, bf16[2,2,576,1024]{3,2,1,0:T(8,128)(2,1)} %collective-permute-done.theirs_in.theirs_grad.theirs, ...), custom_call_target="tpu_custom_call" | custom-call | flops 1 | bytes 1 | tf_op jit(solution)/shard_map/expert/pallas_call | solution.py:159
  207.2 2.4 copy.35
  209.6 2.7 constant_dynamic-slice_fusion.1
  217.0 3.0 collective-permute-start.3
  219.9 3.3 collective-permute-done.3
  223.4 7.9 %collective-permute-done.4 = bf16[128,1024]{1,0:T(8,128)(2,1)S(1)} collective-permute-done((bf16[128,1024]{1,0:T(8,128)(2,1)S(1)}, bf16[128,1024]{1,0:T(8,128)(2,1)S(1)}, u32[]{:S(2)}, u32[]{:S(2)}) %collective-permute-start.4) | collective-permute-done | bytes 262176 | tf_op jit(solution)/shard_map/ppermute | solution.py:304
  232.0 2.2 collective-permute-start.5
  234.2 5.8 %collective-permute-done.5 = bf16[128,1024]{1,0:T(8,128)(2,1)} collective-permute-done((bf16[128,1024]{1,0:T(8,128)(2,1)S(1)}, bf16[128,1024]{1,0:T(8,128)(2,1)}, u32[]{:S(2)}, u32[]{:S(2)}) %collective-permute-start.5) | collective-permute-done | bytes 262176 | tf_op jit(solution)/shard_map/ppermute | solution.py:304
  242.1 4.1 %copy.37.refs_3_.refs_5_.refs_7_ = bf16[3,1024,344]{2,1,0:T(8,128)(2,1)} copy(bf16[3,1024,344]{1,2,0:T(8,128)(2,1)} %collective-permute-done.1) | data formatting | bytes 4227072 | tf_op jit(solution)/shard_map/ppermute | solution.py:241
  249.7 7.1 %token_partial.2 = bf16[2,1024,1024]{2,1,0:T(8,128)(2,1)} custom-call(s32[1]{0:T(128)} %bitcast.core_ref.refs_0_, bf16[3,1024,344]{2,1,0:T(8,128)(2,1)S(1)} %get-tuple-element.39.refs_1_.refs_3_, bf16[32,344,128]{2,1,0:T(8,128)(2,1)S(1)} %copy-done.11, bf16[3,1024,344]{2,1,0:T(8,128)(2,1)S(1)} %copy-done.2, bf16[16,344,128]{2,1,0:T(8,128)(2,1)} %collective-permute-done.2.refs_4_), custom_call_target="tpu_custom_call" | custom-call | flops 1 | bytes 1 | tf_op jit(solution)/shard_map/token_partial/pallas_call | solution.py:229
  256.8 7.0 %all-to-all-start.4 = ((bf16[64,32,1024]{2,1,0:T(8,128)(2,1)}), bf16[64,32,1024]{2,1,0:T(8,128)(2,1)}, u32[]{:S(2)}, u32[]{:S(2)}) async-start(bf16[64,32,1024]{2,1,0:T(8,128)(2,1)} %bitcast.37), calls=%async_computation.4 | async-start | bytes 8388608 | tf_op jit(solution)/shard_map/all_to_all | solution.py:253
  263.7 2.3 copy-done.1
  266.1 5.6 %weight_grads.3 = bf16[4096,344]{1,0:T(8,128)(2,1)S(1)} custom-call(s32[1]{0:T(128)} %bitcast.core_ref.refs_0_, bf16[2,2,576,1024]{3,2,1,0:T(8,128)(2,1)S(1)} %copy-done.1, bf16[2,2,576,1024]{3,2,1,0:T(8,128)(2,1)} %collective-permute-done.theirs_in.theirs_grad.theirs, bf16[576,344]{1,0:T(8,128)(2,1)S(1)} %get-tuple-element.48.refs_0_), custom_call_target="tpu_custom_call" | custom-call | flops 1 | bytes 1 | tf_op jit(solution)/shard_map/weight_grads/pallas_call | solution.py:190
  273.4 8.7 %weight_grads.2 = (bf16[4096,344]{1,0:T(8,128)(2,1)S(1)}, bf16[4096,344]{1,0:T(8,128)(2,1)S(1)}) custom-call(s32[1]{0:T(128)} %bitcast.core_ref.refs_0_, bf16[2,2,576,1024]{3,2,1,0:T(8,128)(2,1)} %copy-done, bf16[2,2,576,1024]{3,2,1,0:T(8,128)(2,1)} %collective-permute-done.theirs_in.theirs_grad.theirs, bf16[576,344]{1,0:T(8,128)(2,1)S(1)} %get-tuple-element.44.refs_0_, ...), custom_call_target="tpu_custom_call" | custom-call | flops 1 | bytes 1 | tf_op jit(solution)/shard_map/weight_grads/pallas_call | solution.py:190
  283.8 12.5 %token_partial.3 = bf16[2,1024,1024]{2,1,0:T(8,128)(2,1)} custom-call(s32[1]{0:T(128)} %bitcast.core_ref.refs_0_, bf16[3,1024,344]{2,1,0:T(8,128)(2,1)S(1)} %get-tuple-element.39.refs_1_.refs_3_, bf16[32,344,128]{2,1,0:T(8,128)(2,1)S(1)} %copy-done.6, bf16[3,1024,344]{2,1,0:T(8,128)(2,1)S(1)} %get-tuple-element.39.refs_1_.refs_3_, ...), custom_call_target="tpu_custom_call" | custom-call | flops 1 | bytes 1 | tf_op jit(solution)/shard_map/token_partial/pallas_call | solution.py:229
  296.4 23.7 %all-to-all-done.4 = bf16[64,32,1024]{2,1,0:T(8,128)(2,1)} async-done(((bf16[64,32,1024]{2,1,0:T(8,128)(2,1)}), bf16[64,32,1024]{2,1,0:T(8,128)(2,1)}, u32[]{:S(2)}, u32[]{:S(2)}) %all-to-all-start.4) | async-done | bytes 4194336 | tf_op jit(solution)/shard_map/all_to_all | solution.py:253
  320.1 9.4 %all-to-all-start.3 = ((bf16[64,32,1024]{2,1,0:T(8,128)(2,1)}), bf16[64,32,1024]{2,1,0:T(8,128)(2,1)}, u32[]{:S(2)}, u32[]{:S(2)}) async-start(bf16[64,32,1024]{2,1,0:T(8,128)(2,1)} %bitcast.36), calls=%async_computation.3 | async-start | bytes 8388608 | tf_op jit(solution)/shard_map/all_to_all | solution.py:253
  329.5 2.8 copy.42
  332.3 4.7 %copy.43 = bf16[1,4096,344]{1,2,0:T(8,128)(2,1)} copy(bf16[1,4096,344]{2,1,0:T(8,128)(2,1)} %bitcast.31) | data formatting | bytes 5636096
  337.0 2.8 copy.44
  339.7 3.7 reduce_sum.64
  343.4 43.2 %all-to-all-done.3 = bf16[64,32,1024]{2,1,0:T(8,128)(2,1)} async-done(((bf16[64,32,1024]{2,1,0:T(8,128)(2,1)}), bf16[64,32,1024]{2,1,0:T(8,128)(2,1)}, u32[]{:S(2)}, u32[]{:S(2)}) %all-to-all-start.3) | async-done | bytes 4194336 | tf_op jit(solution)/shard_map/all_to_all | solution.py:253
  386.6 3.7 reduce_sum.65
  (106 shorter events, 34.9 us)
Async XLA Ops:
  7.2 165.1 %all-gather.2.cloned.1.call-start = ((), (), s32[]{:S(2)}) async-start(), calls=%async_computation.5 | async-start | bytes 9052160 | tf_op jit(solution)/shard_map/all_gather | solution.py:322
  10.3 1.8 copy-start.20
  14.7 45.1 %all-to-all-start = ((bf16[32,344,128]{2,1,0:T(8,128)(2,1)}), bf16[32,344,128]{2,1,0:T(8,128)(2,1)S(1)}, u32[]{:S(2)}, u32[]{:S(2)}) async-start(bf16[32,344,128]{2,1,0:T(8,128)(2,1)} %bitcast.29), calls=%async_computation | async-start | bytes 5636096 | tf_op jit(solution)/shard_map/all_to_all | solution.py:59
  24.5 1.9 copy-start.21
  26.4 2.6 copy-start.22
  59.8 47.8 %copy-start.4 = (bf16[32,344,128]{2,1,0:T(8,128)(2,1)}, bf16[32,344,128]{2,1,0:T(8,128)(2,1)S(1)}, u32[]{:S(2)}) copy-start(bf16[32,344,128]{2,1,0:T(8,128)(2,1)S(1)} %all-to-all-done.gate_cols.refs_2_) | copy-start | bytes 8454148
  107.5 60.4 %all-to-all-start.2 = ((bf16[32,344,128]{2,1,0:T(8,128)(2,1)}), bf16[32,344,128]{2,1,0:T(8,128)(2,1)S(1)}, u32[]{:S(2)}, u32[]{:S(2)}) async-start(bf16[32,344,128]{2,1,0:T(8,128)(2,1)} %bitcast.28), calls=%async_computation.2 | async-start | bytes 5636096 | tf_op jit(solution)/shard_map/all_to_all | solution.py:59
  167.9 14.6 %copy-start.9 = (bf16[32,344,128]{2,1,0:T(8,128)(2,1)}, bf16[32,344,128]{2,1,0:T(8,128)(2,1)S(1)}, u32[]{:S(2)}) copy-start(bf16[32,344,128]{2,1,0:T(8,128)(2,1)S(1)} %all-to-all-done.2.down_cols.refs_2_) | copy-start | bytes 8454148
  182.5 9.2 %collective-permute-start = (bf16[2,2,576,1024]{3,2,1,0:T(8,128)(2,1)}, bf16[2,2,576,1024]{3,2,1,0:T(8,128)(2,1)}, u32[]{:S(2)}, u32[]{:S(2)}) collective-permute-start(bf16[2,2,576,1024]{3,2,1,0:T(8,128)(2,1)} %pick_rows.3), channel_id=1, source_target_pairs={{0,32},{32,0},{1,33},{33,1},{2,34},{34,2},{3,35},{35,3},{4,36},{36... | collective-permute-start | bytes 14155784 | tf_op jit(solution)/shard_map/ppermute | solution.py:241
  183.7 8.0 %copy-start.5 = (bf16[32,344,128]{2,1,0:T(8,128)(2,1)S(1)}, bf16[32,344,128]{2,1,0:T(8,128)(2,1)}, u32[]{:S(2)}) copy-start(bf16[32,344,128]{2,1,0:T(8,128)(2,1)} %copy-done.4) | copy-start | bytes 8454148
  183.8 8.0 %copy-start.7 = (bf16[32,344,128]{2,1,0:T(8,128)(2,1)S(1)}, bf16[32,344,128]{2,1,0:T(8,128)(2,1)}, u32[]{:S(2)}) copy-start(bf16[32,344,128]{2,1,0:T(8,128)(2,1)} %all_to_all.25.up_cols.refs_4_) | copy-start | bytes 8454148
  189.4 2.1 copy-start
  209.6 32.5 %collective-permute-start.1 = (bf16[3,1024,344]{1,2,0:T(8,128)(2,1)}, bf16[3,1024,344]{1,2,0:T(8,128)(2,1)}, u32[]{:S(2)}, u32[]{:S(2)}) collective-permute-start(bf16[3,1024,344]{1,2,0:T(8,128)(2,1)} %copy.35), channel_id=1, source_target_pairs={{0,32},{32,0},{1,33},{33,1},{2,34},{34,2},{3,35},{35,3},{4,36},{36... | collective-permute-start | bytes 6340616 | tf_op jit(solution)/shard_map/ppermute | solution.py:241
  209.6 3.2 copy-start.10
  209.6 4.4 %copy-start.8 = (bf16[32,344,128]{2,1,0:T(8,128)(2,1)S(1)}, bf16[32,344,128]{2,1,0:T(8,128)(2,1)}, u32[]{:S(2)}) copy-start(bf16[32,344,128]{2,1,0:T(8,128)(2,1)} %all_to_all.25.up_cols.refs_4_) | copy-start | bytes 8454148
  212.3 44.5 %collective-permute-start.6 = (bf16[16,344,128]{2,1,0:T(8,128)(2,1)}, bf16[16,344,128]{2,1,0:T(8,128)(2,1)}, u32[]{:S(2)}, u32[]{:S(2)}) collective-permute-start(bf16[16,344,128]{2,1,0:T(8,128)(2,1)} %bitcast.10), channel_id=1, source_target_pairs={{0,32},{32,0},{1,33},{33,1},{2,34},{34,2},{3,35},{35,3},{4,36},{36... | collective-permute-start | bytes 4227080 | tf_op jit(solution)/shard_map/ppermute | solution.py:241
  214.0 32.2 %collective-permute-start.2 = (bf16[16,344,128]{2,1,0:T(8,128)(2,1)}, bf16[16,344,128]{2,1,0:T(8,128)(2,1)}, u32[]{:S(2)}, u32[]{:S(2)}) collective-permute-start(bf16[16,344,128]{2,1,0:T(8,128)(2,1)} %bitcast.8), channel_id=1, source_target_pairs={{0,32},{32,0},{1,33},{33,1},{2,34},{34,2},{3,35},{35,3},{4,36},{36... | collective-permute-start | bytes 4227080 | tf_op jit(solution)/shard_map/ppermute | solution.py:241
  215.3 41.5 %collective-permute-start.7 = (bf16[16,344,128]{2,1,0:T(8,128)(2,1)}, bf16[16,344,128]{2,1,0:T(8,128)(2,1)}, u32[]{:S(2)}, u32[]{:S(2)}) collective-permute-start(bf16[16,344,128]{2,1,0:T(8,128)(2,1)} %bitcast.12), channel_id=1, source_target_pairs={{0,32},{32,0},{1,33},{33,1},{2,34},{34,2},{3,35},{35,3},{4,36},{36... | collective-permute-start | bytes 4227080 | tf_op jit(solution)/shard_map/ppermute | solution.py:241
  217.0 6.3 %collective-permute-start.3 = (bf16[128,1024]{1,0:T(8,128)(2,1)S(1)}, bf16[128,1024]{1,0:T(8,128)(2,1)S(1)}, u32[]{:S(2)}, u32[]{:S(2)}) collective-permute-start(bf16[128,1024]{1,0:T(8,128)(2,1)S(1)} %get-tuple-element.79), channel_id=1, source_target_pairs={{0,32},{32,64},{64,96},{96,0},{1,33},{33,65},{65,97},{97,1},{2,34}... | collective-permute-start | bytes 786440 | tf_op jit(solution)/shard_map/ppermute | solution.py:304
  223.3 8.1 %copy-start.25 = (bf16[128,1024]{1,0:T(8,128)(2,1)}, bf16[128,1024]{1,0:T(8,128)(2,1)S(1)}, u32[]{:S(2)}) copy-start(bf16[128,1024]{1,0:T(8,128)(2,1)S(1)} %collective-permute-done.3) | copy-start | bytes 786436
  223.3 8.1 %collective-permute-start.4 = (bf16[128,1024]{1,0:T(8,128)(2,1)S(1)}, bf16[128,1024]{1,0:T(8,128)(2,1)S(1)}, u32[]{:S(2)}, u32[]{:S(2)}) collective-permute-start(bf16[128,1024]{1,0:T(8,128)(2,1)S(1)} %get-tuple-element.81), channel_id=1, source_target_pairs={{0,64},{32,96},{64,0},{96,32},{1,65},{33,97},{65,1},{97,33},{2,66}... | collective-permute-start | bytes 786440 | tf_op jit(solution)/shard_map/ppermute | solution.py:304
  232.0 8.0 %collective-permute-start.5 = (bf16[128,1024]{1,0:T(8,128)(2,1)S(1)}, bf16[128,1024]{1,0:T(8,128)(2,1)}, u32[]{:S(2)}, u32[]{:S(2)}) collective-permute-start(bf16[128,1024]{1,0:T(8,128)(2,1)S(1)} %get-tuple-element.80), channel_id=1, source_target_pairs={{0,96},{32,0},{64,32},{96,64},{1,97},{33,1},{65,33},{97,65},{2,98}... | collective-permute-start | bytes 786440 | tf_op jit(solution)/shard_map/ppermute | solution.py:304
  247.9 1.8 copy-start.11
  256.8 63.3 %all-to-all-start.4 = ((bf16[64,32,1024]{2,1,0:T(8,128)(2,1)}), bf16[64,32,1024]{2,1,0:T(8,128)(2,1)}, u32[]{:S(2)}, u32[]{:S(2)}) async-start(bf16[64,32,1024]{2,1,0:T(8,128)(2,1)} %bitcast.37), calls=%async_computation.4 | async-start | bytes 8388608 | tf_op jit(solution)/shard_map/all_to_all | solution.py:253
  263.7 2.3 copy-start.1
  266.1 7.3 %copy-start.24 = (bf16[576,344]{1,0:T(8,128)(2,1)S(1)}, bf16[576,344]{1,0:T(8,128)(2,1)}, u32[]{:S(2)}) copy-start(bf16[576,344]{1,0:T(8,128)(2,1)} %copy-done.23) | copy-start | bytes 1188868
  273.4 10.5 %copy-start.3 = (bf16[3,1024,344]{2,1,0:T(8,128)(2,1)S(1)}, bf16[3,1024,344]{2,1,0:T(8,128)(2,1)}, u32[]{:S(2)}) copy-start(bf16[3,1024,344]{2,1,0:T(8,128)(2,1)} %copy.37.refs_3_.refs_5_.refs_7_) | copy-start | bytes 6340612
  273.4 10.5 %copy-start.6 = (bf16[32,344,128]{2,1,0:T(8,128)(2,1)S(1)}, bf16[32,344,128]{2,1,0:T(8,128)(2,1)}, u32[]{:S(2)}) copy-start(bf16[32,344,128]{2,1,0:T(8,128)(2,1)} %copy-done.4) | copy-start | bytes 8454148
  283.8 12.5 %copy-start.17 = (bf16[4096,344]{1,0:T(8,128)(2,1)}, bf16[4096,344]{1,0:T(8,128)(2,1)S(1)}, u32[]{:S(2)}) copy-start(bf16[4096,344]{1,0:T(8,128)(2,1)S(1)} %get-tuple-element.54) | copy-start | bytes 8454148
  320.1 9.4 %copy-start.19 = (bf16[4096,344]{1,0:T(8,128)(2,1)S(1)}, bf16[4096,344]{1,0:T(8,128)(2,1)}, u32[]{:S(2)}) copy-start(bf16[4096,344]{1,0:T(8,128)(2,1)} %copy-done.18) | copy-start | bytes 8454148
  320.1 66.5 %all-to-all-start.3 = ((bf16[64,32,1024]{2,1,0:T(8,128)(2,1)}), bf16[64,32,1024]{2,1,0:T(8,128)(2,1)}, u32[]{:S(2)}, u32[]{:S(2)}) async-start(bf16[64,32,1024]{2,1,0:T(8,128)(2,1)} %bitcast.36), calls=%async_computation.3 | async-start | bytes 8388608 | tf_op jit(solution)/shard_map/all_to_all | solution.py:253
  332.3 4.7 %copy-start.13 = (bf16[4096,344]{1,0:T(8,128)(2,1)S(1)}, bf16[4096,344]{1,0:T(8,128)(2,1)}, u32[]{:S(2)}) copy-start(bf16[4096,344]{1,0:T(8,128)(2,1)} %copy-done.12) | copy-start | bytes 8454148
  (8 other events, 11.2 us)
Sparse Core Ops, SparseCore 0:
  11.4 160.7 all-gather.1

commit v2 on v1

--- a/solution.py
+++ b/solution.py
@@ -1,3 +1,6 @@
+import functools
+import itertools
+
 import jax
 import jax.numpy as jnp
 from jax import lax
@@ -16,7 +19,10 @@
 PLANE = ("xh", "xl", "z", "y")
 CONTRACT_LAST = (((1,), (1,)), ((), ()))
 CONTRACT_FIRST = (((0,), (0,)), ((), ()))
-VMEM = 44 * 2**20
+VMEM = 56 * 2**20
+RING = 4
+AXES = "xzy"
+PARTS = ((0, 512, "xzy"), (512, 1024, "zyx"))
 
 
 def call(kernel, prefetch, grid, ins, outs, shapes, name, scratch=()):
@@ -93,8 +99,9 @@
 
 def spread_tokens(spread_ref, values, o_ref):
     slots, per = spread_ref.shape[2], spread_ref.shape[1]
+    rest = jnp.zeros((slots, o_ref.shape[1] - values.shape[1]), BF)
     for g in range(GROUPS):
-        part = values[g * slots : (g + 1) * slots]
+        part = jnp.concatenate([values[g * slots : (g + 1) * slots], rest], axis=1)
         rows = jnp.dot(spread_ref[g], part, preferred_element_type=F32)
         o_ref[pl.ds(g * per, per), :] = rows.astype(BF)
 
@@ -152,7 +159,7 @@
 def expert(core, mine, theirs, gate_cols, up_cols, down_cols, slot_gate, spread):
     total, width = mine.shape[2:]
     blocks, units, depth = gate_cols.shape
-    tokens = spread.shape[0] * spread.shape[1]
+    by_token = (3, spread.shape[0] * spread.shape[1], -(-units // 128) * 128)
     cols = pl.BlockSpec(
         (blocks // 4, units, depth), lambda h, x, c: (2 * x + jnp.where(h == 0, c[0], 1 - c[0]), 0, 0)
     )
@@ -164,9 +171,9 @@
         + row_specs(1, total, width)
         + [cols] * 3
         + [whole(slot_gate.shape), whole(spread.shape)],
-        [whole((total, units))] * 3 + [whole((3, tokens, units))],
+        [whole((total, units))] * 3 + [whole(by_token)],
         [jax.ShapeDtypeStruct((total, units), BF)] * 3
-        + [jax.ShapeDtypeStruct((3, tokens, units), BF)],
+        + [jax.ShapeDtypeStruct(by_token, BF)],
         "expert",
         scratch=[pltpu.VMEM((total, units), F32)] * 3,
     )(core, mine, theirs, mine, theirs, gate_cols, up_cols, down_cols, slot_gate, spread)
@@ -176,7 +183,7 @@
     count = len(refs) // 2
     rows = jnp.where(pl.program_id(0) == 0, mine[0, 0], theirs[0, 0])
     for delta, out in zip(refs[:count], refs[count:]):
-        grad = lax.dot_general(rows, delta[...], CONTRACT_FIRST, preferred_element_type=F32)
+        grad = lax.dot_general(delta[...], rows, CONTRACT_FIRST, preferred_element_type=F32)
         out[...] = grad.astype(BF)
 
 
@@ -185,7 +192,7 @@
     units = deltas[0].shape[1]
     rows = row_specs(which, total, width)
     out = pl.BlockSpec(
-        (width, units), lambda h, x, c: (2 * x + jnp.where(h == 0, c[0], 1 - c[0]), 0)
+        (units, width), lambda h, x, c: (0, 2 * x + jnp.where(h == 0, c[0], 1 - c[0]))
     )
     return call(
         weight_grad_kernel,
@@ -193,48 +200,147 @@
         (2, 2),
         rows + [whole(d.shape) for d in deltas],
         [out] * len(deltas),
-        [jax.ShapeDtypeStruct((4 * width, units), BF)] * len(deltas),
+        [jax.ShapeDtypeStruct((units, 4 * width), BF)] * len(deltas),
         "weight_grads",
     )(core, mine, theirs, *deltas)
 
 
-def partial_kernel(terms, half_ref, *refs):
-    o_ref = refs[-1]
-    step = 2
-    for first in range(0, refs[1].shape[0], step):
-        total = None
-        for i in range(terms):
-            part = jnp.dot(
-                refs[2 * i][...], wide(refs[2 * i + 1], first, step), preferred_element_type=F32
-            )
-            total = part if total is None else total + part
-        at = pl.ds(first * refs[1].shape[2], step * refs[1].shape[2])
-        o_ref[0, :, at] = total.astype(BF)
-
-
-def token_partial(terms, half):
-    _, tokens, units = terms[0][0].shape
-    blocks, _, depth = terms[0][2].shape
+def spots(left, axis):
+    strides = {name: RING ** (len(left) - 1 - i) for i, name in enumerate(left)}
+    others = [name for name in left if name != axis]
+    for number, places in enumerate(itertools.product(range(RING), repeat=len(others))):
+        yield number, sum(p * strides[o] for p, o in zip(places, others)), strides[axis]
+
+
+def along(place_ref, axis, shift):
+    return lax.rem(place_ref[1 + AXES.index(axis)] + shift, RING)
+
+
+def cut(left, part, stage, place_ref, load, pieces):
+    axis = PARTS[part][2][stage]
+    for shift, piece in enumerate(pieces):
+        there = along(place_ref, axis, shift)
+        for number, base, stride in spots(left, axis):
+            load(base + stride * there, piece, number)
+
+
+def sums_kernel(place_ref, mine, theirs, gate, up, down, their_gate, their_up, their_down, *refs):
+    pieces, whole_ref = refs[:-1], refs[-1]
+    x, n = pl.program_id(0), pl.program_id(1)
+    units, step = gate.shape[1], 2
+    outputs = (
+        ((0, down, their_down),),
+        ((1, gate, their_gate), (2, up, their_up)),
+    )
+    for first in range(0, gate.shape[0], step):
+        at = slice(first * gate.shape[2], (first + step) * gate.shape[2])
+        for t, terms in enumerate(outputs):
+            total = None
+            for i, own, other in terms:
+                for rows, weight in ((mine, own), (theirs, other)):
+                    part = jnp.dot(
+                        rows[i, :, :units], wide(weight, first, step), preferred_element_type=F32
+                    )
+                    total = part if total is None else total + part
+            rows_of = whole_ref.shape[3]
+            total = total.reshape(-1, rows_of, total.shape[1]).astype(BF)
+            whole_ref[t, n, pl.ds(x * total.shape[0], total.shape[0]), :, at] = total
+
+    @pl.when((x == 1) & (n == 1))
+    def _():
+        half = whole_ref.shape[4]
+        for p, (low, high, _) in enumerate(PARTS):
+
+            def load(spot, piece, number):
+                for t in range(2):
+                    for m in range(2):
+                        lo, hi = max(low, m * half), min(high, (m + 1) * half)
+                        if lo < hi:
+                            piece[t, number, :, lo - low : hi - low] = whole_ref[
+                                t, m, spot, :, lo - m * half : hi - m * half
+                            ]
+
+            cut(AXES, p, 0, place_ref, load, pieces[RING * p : RING * (p + 1)])
+
+
+def piece_shapes(stage, rows):
+    spots_left = (RING ** (2 - stage),) if stage < 2 else ()
+    return [
+        jax.ShapeDtypeStruct((2,) + spots_left + (rows, high - low), BF)
+        for low, high, _ in PARTS
+        for _ in range(RING)
+    ]
+
+
+def first_pieces(place, mine, theirs, cols, their_cols):
+    _, tokens, padded = mine.shape
+    blocks, units, depth = cols[0].shape
     per = blocks // 8
-    quarter = 2 * per * depth
-    specs, args = [], []
-    for rows, i, weight in terms:
-        specs.append(pl.BlockSpec((None, tokens, units), lambda x, n, h, i=i: (i, 0, 0)))
-        if weight.shape[0] == blocks:
-            index = lambda x, n, h: (4 * x + 2 * h[0] + n, 0, 0)
-        else:
-            index = lambda x, n, h: (2 * x + n, 0, 0)
-        specs.append(pl.BlockSpec((per, units, depth), index))
-        args += [rows, weight]
+    rows = tokens // BLK
+    shapes = piece_shapes(0, rows)
     return call(
-        lambda *refs: partial_kernel(len(terms), *refs),
+        sums_kernel,
         1,
         (2, 2),
-        specs,
-        pl.BlockSpec((1, tokens, per * depth), lambda x, n, h: (x, 0, n)),
-        jax.ShapeDtypeStruct((2, tokens, quarter), BF),
-        "token_partial",
-    )(half, *args)
+        [whole(mine.shape)] * 2
+        + [pl.BlockSpec((per, units, depth), lambda x, n, c: (4 * x + 2 * c[0] + n, 0, 0))] * 3
+        + [pl.BlockSpec((per, units, depth), lambda x, n, c: (2 * x + n, 0, 0))] * 3,
+        [whole(shape.shape) for shape in shapes],
+        shapes,
+        "token_sums",
+        scratch=[pltpu.VMEM((2, 2, 2 * BLK, rows, per * depth), BF)],
+    )(place, mine, theirs, *cols, *their_cols)
+
+
+def add_kernel(stage, place_ref, *refs):
+    gathered, outs = refs[: RING * len(PARTS)], refs[RING * len(PARTS) :]
+    for p, (low, high, order) in enumerate(PARTS):
+        group = gathered[RING * p : RING * (p + 1)]
+
+        def summed(*spot):
+            return sum(ref[spot].astype(F32) for ref in group).astype(BF)
+
+        if stage == 3:
+            for t in range(2):
+                outs[t][:, low:high] = summed(t)
+            continue
+        left = [name for name in AXES if name not in order[:stage]]
+
+        def load(spot, piece, number):
+            for t in range(2):
+                if stage == 1:
+                    piece[t, number] = summed(t, spot)
+                else:
+                    piece[t] = summed(t, spot)
+
+        cut(left, p, stage, place_ref, load, outs[RING * p : RING * (p + 1)])
+
+
+def add_pieces(stage, place, gathered):
+    rows = gathered[0].shape[-2]
+    if stage == 3:
+        shapes = [jax.ShapeDtypeStruct((rows, PARTS[-1][1]), BF)] * 2
+    else:
+        shapes = piece_shapes(stage, rows)
+    return call(
+        functools.partial(add_kernel, stage),
+        1,
+        (1,),
+        [whole(piece.shape) for piece in gathered],
+        [whole(shape.shape) for shape in shapes],
+        shapes,
+        "add_pieces",
+    )(place, *gathered)
+
+
+def exchanged(stage, pieces):
+    got = list(pieces)
+    for shift in (1, 3, 2):
+        for p, (_, _, order) in enumerate(PARTS):
+            names = {"x": ("xh", "xl")}.get(order[stage], order[stage])
+            there = [(i, (i + shift) % RING) for i in range(RING)]
+            got[RING * p + shift] = lax.ppermute(pieces[RING * p + shift], names, there)
+    return got
 
 
 def over_core(x):
@@ -246,15 +352,6 @@
     cut = cols.reshape(2, 2, blocks // 4, units, depth)
     picked = lax.dynamic_index_in_dim(cut, half, 1, keepdims=False)
     return picked.reshape(blocks // 2, units, depth)
-
-
-def scattered(mine):
-    rows, quarter = mine.shape[1] // BLK, mine.shape[2]
-    return lax.all_to_all(mine.reshape(2 * BLK, rows, quarter), PLANE, 0, 0, tiled=True)
-
-
-def summed(parts):
-    return jnp.sum(parts.astype(F32), axis=0).astype(BF)
 
 
 def route_columns(ids, gates):
@@ -326,12 +423,14 @@
     up_blocks, down_blocks = transposed(up_weight), transposed(down_weight)
     gate_cols = to_owners(gate_blocks)
     gate_cols, up_blocks, down_blocks = together(gate_cols, up_blocks, down_blocks)
+    their_gate = over_core(half_blocks(gate_cols, 1 - core))
     up_cols = to_owners(up_blocks)
     up_cols, down_blocks = together(up_cols, down_blocks)
+    their_up = over_core(half_blocks(up_cols, 1 - core))
     down_cols = to_owners(down_blocks)
-    their_gate = over_core(half_blocks(gate_cols, 1 - core))
-    their_up = over_core(half_blocks(up_cols, 1 - core))
-    down_cols, gathered = together(down_cols, gathered)
+    down_cols, gathered, their_gate, their_up = together(
+        down_cols, gathered, their_gate, their_up
+    )
 
     ids, gates = routes(gathered[0, :, :, 2 * width :])
     selector, spread, slot_gate = slot_tables(ids, gates, expert_id)
@@ -339,41 +438,36 @@
     theirs = over_core(picked_rows(other_selector, other_gate, gathered))
     their_down = over_core(half_blocks(down_cols, 1 - core))
     mine = picked_rows(selector, slot_gate, gathered)
-    attention, mine = together(attention_out[0], mine)
-    merged_attention = average(attention)
+    mine, theirs, their_down = together(mine, theirs, their_down)
     hidden, gate_delta, up_delta, by_token = expert(
         core_id, mine, theirs, gate_cols, up_cols, down_cols, slot_gate, spread
     )
-    their_token = over_core(by_token)
-    total = token_partial([(by_token, 0, down_cols), (their_token, 0, their_down)], core_id)
-    total, merged_attention, their_gate, their_up = together(
-        total, merged_attention, their_gate, their_up
-    )
-    out_parts = scattered(total)
-
-    total = token_partial(
-        [
-            (by_token, 1, gate_cols),
-            (by_token, 2, up_cols),
-            (their_token, 1, their_gate),
-            (their_token, 2, their_up),
-        ],
-        core_id,
-    )
+    their_token, attention = together(over_core(by_token), attention_out[0])
+    merged_attention = average(attention)
+    place = jnp.stack(
+        [core, 2 * lax.axis_index("xh") + lax.axis_index("xl"), lax.axis_index("z"), lax.axis_index("y")]
+    ).astype(jnp.int32)
+    pieces = first_pieces(
+        place,
+        by_token,
+        their_token,
+        (gate_cols, up_cols, down_cols),
+        (their_gate, their_up, their_down),
+    )
+    got = exchanged(0, pieces)
     gate_grads, up_grads = weight_grads(core_id, mine, theirs, 0, [gate_delta, up_delta])
     (down_grads,) = weight_grads(core_id, mine, theirs, 1, [hidden])
-    total, gate_grads, up_grads, down_grads = together(total, gate_grads, up_grads, down_grads)
-    grad_parts = scattered(total)
-    mixed_out = summed(out_parts)
-    grad_parts, mixed_out = together(grad_parts, mixed_out)
-    token_grads = summed(grad_parts)
+    *got, gate_grads, up_grads, down_grads = together(*got, gate_grads, up_grads, down_grads)
+    got = exchanged(1, add_pieces(1, place, got))
+    got = exchanged(2, add_pieces(2, place, got))
+    mixed_out, token_grads = add_pieces(3, place, got)
     return (
         merged_attention,
         mixed_out,
         token_grads,
-        gate_grads[None],
-        up_grads[None],
-        down_grads[None],
+        gate_grads.T[None],
+        up_grads.T[None],
+        down_grads.T[None],
     )
 
 

time: 401 us -> 352 us (0.88)
  waiting for transfers between devices: 171 us -> 126 us
  local copies, waits for them, and re-layouts: 46.1 us -> 11.1 us
  Pallas kernels: 64.2 us -> 89.9 us
  starting transfers between devices: 39.1 us -> 50.1 us
  other arithmetic: 14.9 us -> 10.2 us
    all_to_all x2 -> x0, waiting for transfers between devices: 66.9 us -> none  [scattered(): lax.all_to_all(mine.reshape(2 * BLK, rows, quarter), PLANE, 0, 0, tiled=T...]
    ppermute x0 -> x18, waiting for transfers between devices: none -> 35.5 us  [exchanged(): got[RING * p + shift] = lax.ppermute(pieces[RING * p + shift], names, there)]
    unnamed x58 -> x49, local copies, waits for them, and re-layouts: 31.5 us -> 4.32 us
    ppermute x0 -> x18, starting transfers between devices: none -> 24.6 us  [exchanged(): got[RING * p + shift] = lax.ppermute(pieces[RING * p + shift], names, there)]
    all_to_all x2 -> x0, starting transfers between devices: 16.3 us -> none  [scattered(): lax.all_to_all(mine.reshape(2 * BLK, rows, quarter), PLANE, 0, 0, tiled=T...]
    pallas_call x2 -> x4, Pallas kernels: 19.6 us -> 33.7 us  [the longest x1 21.7 us: first_pieces(): call(sums_kernel, 1, (2, 2), [whole(mine.shape)] * 2 + [pl.BlockSpec((per...]
    ppermute x3, waiting for transfers between devices: 17.1 us -> 4.26 us  [average(): total = total + lax.ppermute(sent, BRANCH, there).astype(F32)]
    reduce_sum x2 -> x0, other arithmetic: 7.32 us -> none  [summed(): return jnp.sum(parts.astype(F32), axis=0).astype(BF)]
  transfers between devices with their start and end apart: 13 -> 29, of which waited for: 8 -> 15; matrix products, arithmetic and copies ran while one was open for 7% -> 3% of each run, Pallas kernels for 11% -> 10%
where the time goes in v2:
time: 352 us; the launch traced here: 351 us
  waiting for transfers between devices  126 us (36%)
  Pallas kernels  89.9 us (26%)
  starting transfers between devices  50.1 us (14%)
  blocking collectives  48.9 us (14%)
  between operations  14.3 us (4%)
  local copies, waits for them, and re-layouts  11.1 us (3%)
  other arithmetic  10.2 us (3%)
    all_to_all x2, waiting for transfers between devices, to_owners(): return lax.all_to_all(blocks, FSDP, 0, 0, tiled=True)  75.2 us
    all_to_all x1, blocking collectives, to_owners(): return lax.all_to_all(blocks, FSDP, 0, 0, tiled=True)  48.9 us
    ppermute x18, waiting for transfers between devices, exchanged(): got[RING * p + shift] = lax.ppermute(pieces[RING * p + shift], names, there)  35.5 us
    ppermute x18, starting transfers between devices, exchanged(): got[RING * p + shift] = lax.ppermute(pieces[RING * p + shift], names, there)  24.6 us
    pallas_call x1, Pallas kernels, first_pieces(): call(sums_kernel, 1, (2, 2), [whole(mine.shape)] * 2 + [pl.BlockSpec((per...  21.7 us
    pallas_call x1, Pallas kernels, expert(): call(expert_kernel, 1, (2, 2), row_specs(0, total, width) + row_specs(1,...  17.8 us
    all_to_all x2, starting transfers between devices, to_owners(): return lax.all_to_all(blocks, FSDP, 0, 0, tiled=True)  15.3 us
    pallas_call x2, Pallas kernels, weight_grads(): call(weight_grad_kernel, 1, (2, 2), rows + [whole(d.shape) for d in delta...  14.7 us
  transfers between devices with their start and end apart: 29, of which 15 were waited for; matrix products, arithmetic and copies ran while one was open for 3% of the time, Pallas kernels for 10%

profile of v2, /device:TPU:1, one launch (start us, length us, event | category | flops | bytes accessed | tf_op | source)
XLA Modules:
  0.0 350.7 jit_solution(15055395397928564655)
XLA Ops:
  10.3 3.3 transpose_weight.3
  13.6 9.8 %all-to-all-start = ((bf16[32,344,128]{2,1,0:T(8,128)(2,1)}), bf16[32,344,128]{2,1,0:T(8,128)(2,1)S(1)}, u32[]{:S(2)}, u32[]{:S(2)}) async-start(bf16[32,344,128]{2,1,0:T(8,128)(2,1)} %bitcast.37), calls=%async_computation | async-start | bytes 5636096 | tf_op jit(solution)/shard_map/all_to_all | solution.py:65
  23.4 3.3 transpose_weight.4
  26.8 3.3 transpose_weight.5
  30.1 28.5 %all-to-all-done.gate_cols.gate = bf16[32,344,128]{2,1,0:T(8,128)(2,1)S(1)} async-done(((bf16[32,344,128]{2,1,0:T(8,128)(2,1)}), bf16[32,344,128]{2,1,0:T(8,128)(2,1)S(1)}, u32[]{:S(2)}, u32[]{:S(2)}) %all-to-all-start) | async-done | bytes 2818080 | tf_op jit(solution)/shard_map/all_to_all | solution.py:65
  58.6 48.9 %all_to_all.15.up_cols.up = bf16[32,344,128]{2,1,0:T(8,128)(2,1)} all-to-all(bf16[32,344,128]{2,1,0:T(8,128)(2,1)} %bitcast.38), channel_id=1, replica_groups=mesh['xh'=2,'c'=2,'xl'=2,'z'=4,'y'=4] {'xl','z','y'}, dimensions={0} | all-to-all | bytes 5636096 | tf_op jit(solution)/shard_map/all_to_all | solution.py:65
  107.5 5.5 %all-to-all-start.2 = ((bf16[32,344,128]{2,1,0:T(8,128)(2,1)}), bf16[32,344,128]{2,1,0:T(8,128)(2,1)}, u32[]{:S(2)}, u32[]{:S(2)}) async-start(bf16[32,344,128]{2,1,0:T(8,128)(2,1)} %bitcast.36), calls=%async_computation.2 | async-start | bytes 5636096 | tf_op jit(solution)/shard_map/all_to_all | solution.py:65
  118.4 1.9 collective-permute-done.1.their_up
  120.4 46.7 %all-to-all-done.2.down_cols.down = bf16[32,344,128]{2,1,0:T(8,128)(2,1)} async-done(((bf16[32,344,128]{2,1,0:T(8,128)(2,1)}), bf16[32,344,128]{2,1,0:T(8,128)(2,1)}, u32[]{:S(2)}, u32[]{:S(2)}) %all-to-all-start.2) | async-done | bytes 2818080 | tf_op jit(solution)/shard_map/all_to_all | solution.py:65
  167.1 4.4 %all-gather.2.cloned.1.call-done = bf16[2048,2176]{1,0:T(8,128)(2,1)} async-done(((bf16[32,2176]{1,0:T(8,128)(2,1)}), bf16[2048,2176]{1,0:T(8,128)(2,1)}) %all-gather.2.cloned.1.call-update) | async-done | bytes 8912912 | tf_op jit(solution)/shard_map/all_gather | solution.py:419
  176.5 6.8 %pick_rows.3 = bf16[2,2,576,1024]{3,2,1,0:T(8,128)(2,1)} custom-call(bf16[4,144,256]{2,1,0:T(8,128)(2,1)} %fusion.1.sel_ref, f32[576,1]{1,0:T(8,128)} %reshape.227.gate_ref, bf16[2,4,256,2176]{3,2,1,0:T(8,128)(2,1)} %bitcast.32), custom_call_target="tpu_custom_call" | custom-call | flops 1 | bytes 1 | tf_op jit(solution)/shard_map/pick_rows/pallas_call | solution.py:85
  187.3 6.8 %pick_rows.2.mine_in.mine_grad.mine = bf16[2,2,576,1024]{3,2,1,0:T(8,128)(2,1)} custom-call(bf16[4,144,256]{2,1,0:T(8,128)(2,1)} %fusion.2.sel_ref, f32[576,1]{1,0:T(8,128)} %reshape.226.gate_ref.slot_gate, bf16[2,4,256,2176]{3,2,1,0:T(8,128)(2,1)} %bitcast.33), custom_call_target="tpu_custom_call" | custom-call | flops 1 | bytes 1 | tf_op jit(solution)/shard_map/pick_rows/pallas_call | solution.py:85
  195.1 17.8 %expert.1 = (bf16[576,344]{1,0:T(8,128)(2,1)}, bf16[576,344]{1,0:T(8,128)(2,1)}, bf16[576,344]{1,0:T(8,128)(2,1)}, bf16[3,1024,384]{2,1,0:T(8,128)(2,1)}) custom-call(s32[1]{0:T(128)} %bitcast.core_ref, bf16[2,2,576,1024]{3,2,1,0:T(8,128)(2,1)} %pick_rows.2.mine_in.mine_grad.mine, ...), custom_call_target="tpu_custom_call" | custom-call | flops 1 | bytes 1 | tf_op jit(solution)/shard_map/expert/pallas_call | solution.py:166
  214.3 3.8 %collective-permute-done.4.theirs = bf16[3,1024,384]{2,1,0:T(8,128)(2,1)S(1)} collective-permute-done((bf16[3,1024,384]{2,1,0:T(8,128)(2,1)}, bf16[3,1024,384]{2,1,0:T(8,128)(2,1)S(1)}, u32[]{:S(2)}, u32[]{:S(2)}) %collective-permute-start.4) | collective-permute-done | bytes 2359328 | tf_op jit(solution)/shard_map/ppermute | solution.py:347
  219.5 21.7 %token_sums.1 = (bf16[2,16,32,512]{3,2,1,0:T(8,128)(2,1)}, bf16[2,16,32,512]{3,2,1,0:T(8,128)(2,1)}, bf16[2,16,32,512]{3,2,1,0:T(8,128)(2,1)}, bf16[2,16,32,512]...) custom-call(s32[4]{0:T(128)} %pad_add_fusion.place_ref, ...), custom_call_target="tpu_custom_call" | custom-call | flops 1 | bytes 1 | tf_op jit(solution)/shard_map/token_sums/pallas_call | solution.py:281
  241.2 2.7 collective-permute-start.10
  244.5 2.4 collective-permute-start.12
  248.1 18.3 %collective-permute-done.10.refs_3_ = bf16[2,16,32,512]{3,2,1,0:T(8,128)(2,1)S(1)} collective-permute-done((bf16[2,16,32,512]{3,2,1,0:T(8,128)(2,1)}, bf16[2,16,32,512]{3,2,1,0:T(8,128)(2,1)S(1)}, u32[]{:S(2)}, u32[]{:S(2)}) %collective-permute-start.10) | collective-permute-done | bytes 1048608 | tf_op jit(solution)/shard_map/ppermute | solution.py:342
  268.3 6.4 %weight_grads.3 = bf16[344,4096]{1,0:T(8,128)(2,1)} custom-call(s32[1]{0:T(128)} %bitcast.core_ref, bf16[2,2,576,1024]{3,2,1,0:T(8,128)(2,1)} %pick_rows.2.mine_in.mine_grad.mine, bf16[2,2,576,1024]{3,2,1,0:T(8,128)(2,1)} %collective-permute-done.2.theirs_in.theirs_grad.theirs, bf16[576,344]{1,0:T(8,128)(2,1)} %get-tuple-element.90.refs_0_), custom_call_target="tpu_custom_call" | custom-call | flops 1 | bytes 1 | tf_op jit(solution)/shard_map/weight_grads/pallas_call | solution.py:197
  274.8 8.3 %weight_grads.2 = (bf16[344,4096]{1,0:T(8,128)(2,1)}, bf16[344,4096]{1,0:T(8,128)(2,1)}) custom-call(s32[1]{0:T(128)} %bitcast.core_ref, bf16[2,2,576,1024]{3,2,1,0:T(8,128)(2,1)} %pick_rows.2.mine_in.mine_grad.mine, bf16[2,2,576,1024]{3,2,1,0:T(8,128)(2,1)} %collective-permute-done.2.theirs_in.theirs_grad.theirs, ...), custom_call_target="tpu_custom_call" | custom-call | flops 1 | bytes 1 | tf_op jit(solution)/shard_map/weight_grads/pallas_call | solution.py:197
  283.0 9.2 %collective-permute-done.12.refs_6_ = bf16[2,16,32,512]{3,2,1,0:T(8,128)(2,1)S(1)} collective-permute-done((bf16[2,16,32,512]{3,2,1,0:T(8,128)(2,1)}, bf16[2,16,32,512]{3,2,1,0:T(8,128)(2,1)S(1)}, u32[]{:S(2)}, u32[]{:S(2)}) %collective-permute-start.12) | collective-permute-done | bytes 1048608 | tf_op jit(solution)/shard_map/ppermute | solution.py:342
  294.9 6.4 %add_pieces.3 = (bf16[2,4,32,512]{3,2,1,0:T(8,128)(2,1)}, bf16[2,4,32,512]{3,2,1,0:T(8,128)(2,1)}, bf16[2,4,32,512]{3,2,1,0:T(8,128)(2,1)}, bf16[2,4,32,512]{3,2...) custom-call(s32[4]{0:T(128)} %pad_add_fusion.place_ref, ...), custom_call_target="tpu_custom_call" | custom-call | flops 1 | bytes 1 | tf_op jit(solution)/shard_map/add_pieces/pallas_call | solution.py:325
  303.1 2.1 collective-permute-start.15
  306.4 2.4 collective-permute-start.18
  311.2 4.8 %collective-permute-done.15.refs_2_ = bf16[2,4,32,512]{3,2,1,0:T(8,128)(2,1)S(1)} collective-permute-done((bf16[2,4,32,512]{3,2,1,0:T(8,128)(2,1)}, bf16[2,4,32,512]{3,2,1,0:T(8,128)(2,1)S(1)}, u32[]{:S(2)}, u32[]{:S(2)}) %collective-permute-start.15) | collective-permute-done | bytes 262176 | tf_op jit(solution)/shard_map/ppermute | solution.py:342
  316.0 3.6 %collective-permute-start.5 = (bf16[128,1024]{1,0:T(8,128)(2,1)}, bf16[128,1024]{1,0:T(8,128)(2,1)S(1)}, u32[]{:S(2)}, u32[]{:S(2)}) collective-permute-start(bf16[128,1024]{1,0:T(8,128)(2,1)} %get-tuple-element.125), channel_id=1, source_target_pairs={{0,32},{32,64},{64,96},{96,0},{1,33},{33,65},{65,97},{97,1},{2,34}... | collective-permute-start | bytes 786440 | tf_op jit(solution)/shard_map/ppermute | solution.py:401
  319.7 2.8 collective-permute-start.6
  323.4 3.1 add_pieces.4
  328.8 1.9 collective-permute-start.22
  330.7 4.1 %collective-permute-done.6 = bf16[128,1024]{1,0:T(8,128)(2,1)S(1)} collective-permute-done((bf16[128,1024]{1,0:T(8,128)(2,1)S(1)}, bf16[128,1024]{1,0:T(8,128)(2,1)S(1)}, u32[]{:S(2)}, u32[]{:S(2)}) %collective-permute-start.6) | collective-permute-done | bytes 262176 | tf_op jit(solution)/shard_map/ppermute | solution.py:401
  335.1 2.4 collective-permute-start.25
  341.4 2.4 add_pieces.5
  (128 shorter events, 40.1 us)
Async XLA Ops:
  7.2 164.3 %all-gather.2.cloned.1.call-start = ((), (), s32[]{:S(2)}) async-start(), calls=%async_computation.3 | async-start | bytes 9052160 | tf_op jit(solution)/shard_map/all_gather | solution.py:419
  13.6 45.0 %all-to-all-start = ((bf16[32,344,128]{2,1,0:T(8,128)(2,1)}), bf16[32,344,128]{2,1,0:T(8,128)(2,1)S(1)}, u32[]{:S(2)}, u32[]{:S(2)}) async-start(bf16[32,344,128]{2,1,0:T(8,128)(2,1)} %bitcast.37), calls=%async_computation | async-start | bytes 5636096 | tf_op jit(solution)/shard_map/all_to_all | solution.py:65
  58.6 54.4 %copy-start = (bf16[32,344,128]{2,1,0:T(8,128)(2,1)}, bf16[32,344,128]{2,1,0:T(8,128)(2,1)S(1)}, u32[]{:S(2)}) copy-start(bf16[32,344,128]{2,1,0:T(8,128)(2,1)S(1)} %all-to-all-done.gate_cols.gate) | copy-start | bytes 8454148
  107.5 59.6 %all-to-all-start.2 = ((bf16[32,344,128]{2,1,0:T(8,128)(2,1)}), bf16[32,344,128]{2,1,0:T(8,128)(2,1)}, u32[]{:S(2)}, u32[]{:S(2)}) async-start(bf16[32,344,128]{2,1,0:T(8,128)(2,1)} %bitcast.36), calls=%async_computation.2 | async-start | bytes 5636096 | tf_op jit(solution)/shard_map/all_to_all | solution.py:65
  114.2 4.2 %collective-permute-start = (bf16[16,344,128]{2,1,0:T(8,128)(2,1)}, bf16[16,344,128]{2,1,0:T(8,128)(2,1)S(1)}, u32[]{:S(2)}, u32[]{:S(2)}) collective-permute-start(bf16[16,344,128]{2,1,0:T(8,128)(2,1)} %bitcast.6), channel_id=1, source_target_pairs={{0,32},{32,0},{1,33},{33,1},{2,34},{34,2},{3,35},{35,3},{4,36},{36... | collective-permute-start | bytes 4227080 | tf_op jit(solution)/shard_map/ppermute | solution.py:347
  115.9 4.5 %collective-permute-start.1 = (bf16[16,344,128]{2,1,0:T(8,128)(2,1)S(1)}, bf16[16,344,128]{2,1,0:T(8,128)(2,1)}, u32[]{:S(2)}, u32[]{:S(2)}) collective-permute-start(bf16[16,344,128]{2,1,0:T(8,128)(2,1)S(1)} %bitcast.40), channel_id=1, source_target_pairs={{0,32},{32,0},{1,33},{33,1},{2,34},{34,2},{3,35},{35,3},{4,36},{36... | collective-permute-start | bytes 4227080 | tf_op jit(solution)/shard_map/ppermute | solution.py:347
  118.4 64.8 %copy-start.3 = (bf16[16,344,128]{2,1,0:T(8,128)(2,1)}, bf16[16,344,128]{2,1,0:T(8,128)(2,1)S(1)}, u32[]{:S(2)}) copy-start(bf16[16,344,128]{2,1,0:T(8,128)(2,1)S(1)} %collective-permute-done.their_gate) | copy-start | bytes 4227076
  183.3 11.9 %collective-permute-start.2 = (bf16[2,2,576,1024]{3,2,1,0:T(8,128)(2,1)}, bf16[2,2,576,1024]{3,2,1,0:T(8,128)(2,1)}, u32[]{:S(2)}, u32[]{:S(2)}) collective-permute-start(bf16[2,2,576,1024]{3,2,1,0:T(8,128)(2,1)} %pick_rows.3), channel_id=1, source_target_pairs={{0,32},{32,0},{1,33},{33,1},{2,34},{34,2},{3,35},{35,3},{4,36},{36... | collective-permute-start | bytes 14155784 | tf_op jit(solution)/shard_map/ppermute | solution.py:347
  185.3 9.9 %collective-permute-start.3 = (bf16[16,344,128]{2,1,0:T(8,128)(2,1)S(1)}, bf16[16,344,128]{2,1,0:T(8,128)(2,1)S(1)}, u32[]{:S(2)}, u32[]{:S(2)}) collective-permute-start(bf16[16,344,128]{2,1,0:T(8,128)(2,1)S(1)} %bitcast.41), channel_id=1, source_target_pairs={{0,32},{32,0},{1,33},{33,1},{2,34},{34,2},{3,35},{35,3},{4,36},{36... | collective-permute-start | bytes 4227080 | tf_op jit(solution)/shard_map/ppermute | solution.py:347
  195.1 17.9 %copy-start.4 = (bf16[16,344,128]{2,1,0:T(8,128)(2,1)}, bf16[16,344,128]{2,1,0:T(8,128)(2,1)S(1)}, u32[]{:S(2)}) copy-start(bf16[16,344,128]{2,1,0:T(8,128)(2,1)S(1)} %collective-permute-done.3.their_down) | copy-start | bytes 4227076
  213.0 5.1 %collective-permute-start.4 = (bf16[3,1024,384]{2,1,0:T(8,128)(2,1)}, bf16[3,1024,384]{2,1,0:T(8,128)(2,1)S(1)}, u32[]{:S(2)}, u32[]{:S(2)}) collective-permute-start(bf16[3,1024,384]{2,1,0:T(8,128)(2,1)} %get-tuple-element.72.mine), channel_id=1, source_target_pairs={{0,32},{32,0},{1,33},{33,1},{2,34},{34,2},{3,35},{35,3},{4,36},{36... | collective-permute-start | bytes 7077896 | tf_op jit(solution)/shard_map/ppermute | solution.py:347
  241.2 25.2 %collective-permute-start.10 = (bf16[2,16,32,512]{3,2,1,0:T(8,128)(2,1)}, bf16[2,16,32,512]{3,2,1,0:T(8,128)(2,1)S(1)}, u32[]{:S(2)}, u32[]{:S(2)}) collective-permute-start(bf16[2,16,32,512]{3,2,1,0:T(8,128)(2,1)} %get-tuple-element.81), channel_id=1, source_target_pairs={{0,80},{16,0},{64,16},{80,64},{1,81},{17,1},{65,17},{81,65},{2,82}... | collective-permute-start | bytes 3145736 | tf_op jit(solution)/shard_map/ppermute | solution.py:342
  244.0 39.1 %collective-permute-start.11 = (bf16[2,16,32,512]{3,2,1,0:T(8,128)(2,1)}, bf16[2,16,32,512]{3,2,1,0:T(8,128)(2,1)S(1)}, u32[]{:S(2)}, u32[]{:S(2)}) collective-permute-start(bf16[2,16,32,512]{3,2,1,0:T(8,128)(2,1)} %get-tuple-element.83), channel_id=1, source_target_pairs={{0,4},{4,8},{8,12},{12,0},{1,5},{5,9},{9,13},{13,1},{2,6},{6,10},{... | collective-permute-start | bytes 3145736 | tf_op jit(solution)/shard_map/ppermute | solution.py:342
  244.5 47.7 %collective-permute-start.12 = (bf16[2,16,32,512]{3,2,1,0:T(8,128)(2,1)}, bf16[2,16,32,512]{3,2,1,0:T(8,128)(2,1)S(1)}, u32[]{:S(2)}, u32[]{:S(2)}) collective-permute-start(bf16[2,16,32,512]{3,2,1,0:T(8,128)(2,1)} %get-tuple-element.84), channel_id=1, source_target_pairs={{0,8},{4,12},{8,0},{12,4},{1,9},{5,13},{9,1},{13,5},{2,10},{6,14},... | collective-permute-start | bytes 3145736 | tf_op jit(solution)/shard_map/ppermute | solution.py:342
  247.0 45.6 %collective-permute-start.13 = (bf16[2,16,32,512]{3,2,1,0:T(8,128)(2,1)}, bf16[2,16,32,512]{3,2,1,0:T(8,128)(2,1)S(1)}, u32[]{:S(2)}, u32[]{:S(2)}) collective-permute-start(bf16[2,16,32,512]{3,2,1,0:T(8,128)(2,1)} %get-tuple-element.85), channel_id=1, source_target_pairs={{0,12},{4,0},{8,4},{12,8},{1,13},{5,1},{9,5},{13,9},{2,14},{6,2},{... | collective-permute-start | bytes 3145736 | tf_op jit(solution)/shard_map/ppermute | solution.py:342
  248.1 44.5 %collective-permute-start.8 = (bf16[2,16,32,512]{3,2,1,0:T(8,128)(2,1)}, bf16[2,16,32,512]{3,2,1,0:T(8,128)(2,1)S(1)}, u32[]{:S(2)}, u32[]{:S(2)}) collective-permute-start(bf16[2,16,32,512]{3,2,1,0:T(8,128)(2,1)} %get-tuple-element.79), channel_id=1, source_target_pairs={{0,16},{16,64},{64,80},{80,0},{1,17},{17,65},{65,81},{81,1},{2,18}... | collective-permute-start | bytes 3145736 | tf_op jit(solution)/shard_map/ppermute | solution.py:342
  266.5 27.5 %collective-permute-start.9 = (bf16[2,16,32,512]{3,2,1,0:T(8,128)(2,1)}, bf16[2,16,32,512]{3,2,1,0:T(8,128)(2,1)S(1)}, u32[]{:S(2)}, u32[]{:S(2)}) collective-permute-start(bf16[2,16,32,512]{3,2,1,0:T(8,128)(2,1)} %get-tuple-element.80), channel_id=1, source_target_pairs={{0,64},{16,80},{64,0},{80,16},{1,65},{17,81},{65,1},{81,17},{2,66}... | collective-permute-start | bytes 3145736 | tf_op jit(solution)/shard_map/ppermute | solution.py:342
  301.4 7.4 %collective-permute-start.14 = (bf16[2,4,32,512]{3,2,1,0:T(8,128)(2,1)}, bf16[2,4,32,512]{3,2,1,0:T(8,128)(2,1)S(1)}, u32[]{:S(2)}, u32[]{:S(2)}) collective-permute-start(bf16[2,4,32,512]{3,2,1,0:T(8,128)(2,1)} %get-tuple-element.100), channel_id=1, source_target_pairs={{0,4},{4,8},{8,12},{12,0},{1,5},{5,9},{9,13},{13,1},{2,6},{6,10},{... | collective-permute-start | bytes 786440 | tf_op jit(solution)/shard_map/ppermute | solution.py:342
  303.1 13.0 %collective-permute-start.15 = (bf16[2,4,32,512]{3,2,1,0:T(8,128)(2,1)}, bf16[2,4,32,512]{3,2,1,0:T(8,128)(2,1)S(1)}, u32[]{:S(2)}, u32[]{:S(2)}) collective-permute-start(bf16[2,4,32,512]{3,2,1,0:T(8,128)(2,1)} %get-tuple-element.101), channel_id=1, source_target_pairs={{0,8},{4,12},{8,0},{12,4},{1,9},{5,13},{9,1},{13,5},{2,10},{6,14},... | collective-permute-start | bytes 786440 | tf_op jit(solution)/shard_map/ppermute | solution.py:342
  305.2 14.4 %collective-permute-start.16 = (bf16[2,4,32,512]{3,2,1,0:T(8,128)(2,1)}, bf16[2,4,32,512]{3,2,1,0:T(8,128)(2,1)S(1)}, u32[]{:S(2)}, u32[]{:S(2)}) collective-permute-start(bf16[2,4,32,512]{3,2,1,0:T(8,128)(2,1)} %get-tuple-element.102), channel_id=1, source_target_pairs={{0,12},{4,0},{8,4},{12,8},{1,13},{5,1},{9,5},{13,9},{2,14},{6,2},{... | collective-permute-start | bytes 786440 | tf_op jit(solution)/shard_map/ppermute | solution.py:342
  305.5 16.9 %collective-permute-start.17 = (bf16[2,4,32,512]{3,2,1,0:T(8,128)(2,1)}, bf16[2,4,32,512]{3,2,1,0:T(8,128)(2,1)S(1)}, u32[]{:S(2)}, u32[]{:S(2)}) collective-permute-start(bf16[2,4,32,512]{3,2,1,0:T(8,128)(2,1)} %get-tuple-element.104), channel_id=1, source_target_pairs={{0,1},{1,2},{2,3},{3,0},{4,5},{5,6},{6,7},{7,4},{8,9},{9,10},{10,1... | collective-permute-start | bytes 786440 | tf_op jit(solution)/shard_map/ppermute | solution.py:342
  306.4 16.1 %collective-permute-start.18 = (bf16[2,4,32,512]{3,2,1,0:T(8,128)(2,1)}, bf16[2,4,32,512]{3,2,1,0:T(8,128)(2,1)S(1)}, u32[]{:S(2)}, u32[]{:S(2)}) collective-permute-start(bf16[2,4,32,512]{3,2,1,0:T(8,128)(2,1)} %get-tuple-element.105), channel_id=1, source_target_pairs={{0,2},{1,3},{2,0},{3,1},{4,6},{5,7},{6,4},{7,5},{8,10},{9,11},{10,... | collective-permute-start | bytes 786440 | tf_op jit(solution)/shard_map/ppermute | solution.py:342
  308.8 13.7 %collective-permute-start.19 = (bf16[2,4,32,512]{3,2,1,0:T(8,128)(2,1)}, bf16[2,4,32,512]{3,2,1,0:T(8,128)(2,1)S(1)}, u32[]{:S(2)}, u32[]{:S(2)}) collective-permute-start(bf16[2,4,32,512]{3,2,1,0:T(8,128)(2,1)} %get-tuple-element.106), channel_id=1, source_target_pairs={{0,3},{1,0},{2,1},{3,2},{4,7},{5,4},{6,5},{7,6},{8,11},{9,8},{10,9... | collective-permute-start | bytes 786440 | tf_op jit(solution)/shard_map/ppermute | solution.py:342
  316.0 12.7 %collective-permute-start.5 = (bf16[128,1024]{1,0:T(8,128)(2,1)}, bf16[128,1024]{1,0:T(8,128)(2,1)S(1)}, u32[]{:S(2)}, u32[]{:S(2)}) collective-permute-start(bf16[128,1024]{1,0:T(8,128)(2,1)} %get-tuple-element.125), channel_id=1, source_target_pairs={{0,32},{32,64},{64,96},{96,0},{1,33},{33,65},{65,97},{97,1},{2,34}... | collective-permute-start | bytes 786440 | tf_op jit(solution)/shard_map/ppermute | solution.py:401
  319.7 15.1 %collective-permute-start.6 = (bf16[128,1024]{1,0:T(8,128)(2,1)S(1)}, bf16[128,1024]{1,0:T(8,128)(2,1)S(1)}, u32[]{:S(2)}, u32[]{:S(2)}) collective-permute-start(bf16[128,1024]{1,0:T(8,128)(2,1)S(1)} %get-tuple-element.127), channel_id=1, source_target_pairs={{0,64},{32,96},{64,0},{96,32},{1,65},{33,97},{65,1},{97,33},{2,66}... | collective-permute-start | bytes 786440 | tf_op jit(solution)/shard_map/ppermute | solution.py:401
  322.5 12.5 %collective-permute-start.7 = (bf16[128,1024]{1,0:T(8,128)(2,1)S(1)}, bf16[128,1024]{1,0:T(8,128)(2,1)}, u32[]{:S(2)}, u32[]{:S(2)}) collective-permute-start(bf16[128,1024]{1,0:T(8,128)(2,1)S(1)} %get-tuple-element.126), channel_id=1, source_target_pairs={{0,96},{32,0},{64,32},{96,64},{1,97},{33,1},{65,33},{97,65},{2,98}... | collective-permute-start | bytes 786440 | tf_op jit(solution)/shard_map/ppermute | solution.py:401
  326.5 8.6 %collective-permute-start.20 = (bf16[2,32,512]{2,1,0:T(8,128)(2,1)}, bf16[2,32,512]{2,1,0:T(8,128)(2,1)S(1)}, u32[]{:S(2)}, u32[]{:S(2)}) collective-permute-start(bf16[2,32,512]{2,1,0:T(8,128)(2,1)} %get-tuple-element.108), channel_id=1, source_target_pairs={{0,1},{1,2},{2,3},{3,0},{4,5},{5,6},{6,7},{7,4},{8,9},{9,10},{10,1... | collective-permute-start | bytes 196616 | tf_op jit(solution)/shard_map/ppermute | solution.py:342
  328.2 11.1 %collective-permute-start.21 = (bf16[2,32,512]{2,1,0:T(8,128)(2,1)}, bf16[2,32,512]{2,1,0:T(8,128)(2,1)S(1)}, u32[]{:S(2)}, u32[]{:S(2)}) collective-permute-start(bf16[2,32,512]{2,1,0:T(8,128)(2,1)} %get-tuple-element.109), channel_id=1, source_target_pairs={{0,2},{1,3},{2,0},{3,1},{4,6},{5,7},{6,4},{7,5},{8,10},{9,11},{10,... | collective-permute-start | bytes 196616 | tf_op jit(solution)/shard_map/ppermute | solution.py:342
  328.8 10.6 %collective-permute-start.22 = (bf16[2,32,512]{2,1,0:T(8,128)(2,1)}, bf16[2,32,512]{2,1,0:T(8,128)(2,1)S(1)}, u32[]{:S(2)}, u32[]{:S(2)}) collective-permute-start(bf16[2,32,512]{2,1,0:T(8,128)(2,1)} %get-tuple-element.110), channel_id=1, source_target_pairs={{0,3},{1,0},{2,1},{3,2},{4,7},{5,4},{6,5},{7,6},{8,11},{9,8},{10,9... | collective-permute-start | bytes 196616 | tf_op jit(solution)/shard_map/ppermute | solution.py:342
  334.8 5.2 %collective-permute-start.23 = (bf16[2,32,512]{2,1,0:T(8,128)(2,1)}, bf16[2,32,512]{2,1,0:T(8,128)(2,1)S(1)}, u32[]{:S(2)}, u32[]{:S(2)}) collective-permute-start(bf16[2,32,512]{2,1,0:T(8,128)(2,1)} %get-tuple-element.112), channel_id=1, source_target_pairs={{0,16},{16,64},{64,80},{80,0},{1,17},{17,65},{65,81},{81,1},{2,18}... | collective-permute-start | bytes 196616 | tf_op jit(solution)/shard_map/ppermute | solution.py:342
  335.0 5.0 %collective-permute-start.24 = (bf16[2,32,512]{2,1,0:T(8,128)(2,1)}, bf16[2,32,512]{2,1,0:T(8,128)(2,1)S(1)}, u32[]{:S(2)}, u32[]{:S(2)}) collective-permute-start(bf16[2,32,512]{2,1,0:T(8,128)(2,1)} %get-tuple-element.113), channel_id=1, source_target_pairs={{0,64},{16,80},{64,0},{80,16},{1,65},{17,81},{65,1},{81,17},{2,66}... | collective-permute-start | bytes 196616 | tf_op jit(solution)/shard_map/ppermute | solution.py:342
  335.1 5.7 %collective-permute-start.25 = (bf16[2,32,512]{2,1,0:T(8,128)(2,1)}, bf16[2,32,512]{2,1,0:T(8,128)(2,1)S(1)}, u32[]{:S(2)}, u32[]{:S(2)}) collective-permute-start(bf16[2,32,512]{2,1,0:T(8,128)(2,1)} %get-tuple-element.114), channel_id=1, source_target_pairs={{0,80},{16,0},{64,16},{80,64},{1,81},{17,1},{65,17},{81,65},{2,82}... | collective-permute-start | bytes 196616 | tf_op jit(solution)/shard_map/ppermute | solution.py:342
  (21 other events, 80.7 us)
Sparse Core Ops, SparseCore 0:
  11.4 159.9 all-gather.1

commit v3 on v2

--- a/solution.py
+++ b/solution.py
@@ -22,6 +22,7 @@
 VMEM = 56 * 2**20
 RING = 4
 AXES = "xzy"
+SHIFTS = (0, 1, 3, 2)
 PARTS = ((0, 512, "xzy"), (512, 1024, "zyx"))
 
 
@@ -216,10 +217,14 @@
     return lax.rem(place_ref[1 + AXES.index(axis)] + shift, RING)
 
 
+def by_part(refs):
+    return list(refs[:RING]), [refs[RING].at[i] for i in range(RING)]
+
+
 def cut(left, part, stage, place_ref, load, pieces):
     axis = PARTS[part][2][stage]
-    for shift, piece in enumerate(pieces):
-        there = along(place_ref, axis, shift)
+    for i, piece in enumerate(pieces):
+        there = along(place_ref, axis, SHIFTS[i]) if part == 0 else i
         for number, base, stride in spots(left, axis):
             load(base + stride * there, piece, number)
 
@@ -260,16 +265,14 @@
                                 t, m, spot, :, lo - m * half : hi - m * half
                             ]
 
-            cut(AXES, p, 0, place_ref, load, pieces[RING * p : RING * (p + 1)])
-
-
-def piece_shapes(stage, rows):
-    spots_left = (RING ** (2 - stage),) if stage < 2 else ()
-    return [
-        jax.ShapeDtypeStruct((2,) + spots_left + (rows, high - low), BF)
-        for low, high, _ in PARTS
-        for _ in range(RING)
-    ]
+            cut(AXES, p, 0, place_ref, load, by_part(pieces)[p])
+
+
+def piece_shapes(rows):
+    lead = (2, RING**2, rows)
+    width = [high - low for low, high, _ in PARTS]
+    first = jax.ShapeDtypeStruct(lead + (width[0],), BF)
+    return [first] * RING + [jax.ShapeDtypeStruct((RING, *lead, width[1]), BF)]
 
 
 def first_pieces(place, mine, theirs, cols, their_cols):
@@ -277,7 +280,7 @@
     blocks, units, depth = cols[0].shape
     per = blocks // 8
     rows = tokens // BLK
-    shapes = piece_shapes(0, rows)
+    shapes = piece_shapes(rows)
     return call(
         sums_kernel,
         1,
@@ -292,55 +295,84 @@
     )(place, mine, theirs, *cols, *their_cols)
 
 
-def add_kernel(stage, place_ref, *refs):
-    gathered, outs = refs[: RING * len(PARTS)], refs[RING * len(PARTS) :]
-    for p, (low, high, order) in enumerate(PARTS):
-        group = gathered[RING * p : RING * (p + 1)]
-
-        def summed(*spot):
-            return sum(ref[spot].astype(F32) for ref in group).astype(BF)
-
-        if stage == 3:
-            for t in range(2):
-                outs[t][:, low:high] = summed(t)
-            continue
-        left = [name for name in AXES if name not in order[:stage]]
-
-        def load(spot, piece, number):
-            for t in range(2):
-                if stage == 1:
-                    piece[t, number] = summed(t, spot)
-                else:
-                    piece[t] = summed(t, spot)
-
-        cut(left, p, stage, place_ref, load, outs[RING * p : RING * (p + 1)])
-
-
-def add_pieces(stage, place, gathered):
-    rows = gathered[0].shape[-2]
-    if stage == 3:
-        shapes = [jax.ShapeDtypeStruct((rows, PARTS[-1][1]), BF)] * 2
-    else:
-        shapes = piece_shapes(stage, rows)
+def added(pieces):
+    return sum(piece.astype(F32) for piece in pieces).astype(BF)
+
+
+def add_first_kernel(place_ref, *refs):
+    pieces, outs = by_part(refs[: RING + 1]), refs[RING + 1 :]
+
+    def load(spot, piece, number):
+        piece[0, number] = added([ref[0, spot] for ref in pieces[0]])
+
+    left = [name for name in AXES if name != PARTS[0][2][0]]
+    cut(left, 0, 1, place_ref, load, outs[:RING])
+    for spot in range(RING**2):
+        outs[RING][spot, 0] = added([ref[0, spot] for ref in pieces[1]])
+
+
+def add_second_kernel(place_ref, *refs):
+    pieces, outs = refs[:RING], refs[RING:]
+
+    def load(spot, piece, number):
+        piece[0] = added([ref[0, spot] for ref in pieces])
+
+    cut([PARTS[0][2][2]], 0, 2, place_ref, load, outs)
+
+
+def add_last_kernel(place_ref, *refs):
+    pieces, second, out = refs[:RING], refs[RING], refs[RING + 1]
+    (low, middle, _), (_, high, _) = PARTS
+    out[0, :, low:middle] = added([ref[0] for ref in pieces])
+    out[0, :, middle:high] = added([second[i, 0] for i in range(second.shape[0])])
+
+
+def each_result(kernel, place, arrays, shapes):
+    def spec(shape, stacked):
+        if stacked:
+            return pl.BlockSpec(
+                (shape[0], 1, *shape[2:]), lambda t, *_: (0, t) + (0,) * (len(shape) - 2)
+            )
+        return pl.BlockSpec((1, *shape[1:]), lambda t, *_: (t,) + (0,) * (len(shape) - 1))
+
     return call(
-        functools.partial(add_kernel, stage),
+        kernel,
         1,
-        (1,),
-        [whole(piece.shape) for piece in gathered],
-        [whole(shape.shape) for shape in shapes],
+        (2,),
+        [spec(array.shape, i >= RING) for i, array in enumerate(arrays)],
+        [spec(shape.shape, i >= RING) for i, shape in enumerate(shapes)],
         shapes,
         "add_pieces",
-    )(place, *gathered)
-
-
-def exchanged(stage, pieces):
-    got = list(pieces)
-    for shift in (1, 3, 2):
-        for p, (_, _, order) in enumerate(PARTS):
-            names = {"x": ("xh", "xl")}.get(order[stage], order[stage])
-            there = [(i, (i + shift) % RING) for i in range(RING)]
-            got[RING * p + shift] = lax.ppermute(pieces[RING * p + shift], names, there)
+    )(place, *arrays)
+
+
+def axes_of(order):
+    return sum(({"x": ("xh", "xl")}.get(name, (name,)) for name in order), ())
+
+
+def to_shifts(stage, pieces):
+    got = [pieces[0]]
+    for piece, shift in zip(pieces[1:], SHIFTS[1:]):
+        there = [(j, (j + shift) % RING) for j in range(RING)]
+        got.append(lax.ppermute(piece, axes_of(PARTS[0][2][stage]), there))
     return got
+
+
+def reduced(place, pieces):
+    rows, width = pieces[0].shape[-2:]
+    other = PARTS[1][1] - PARTS[1][0]
+    one = jax.ShapeDtypeStruct((2, RING, rows, width), BF)
+    many = jax.ShapeDtypeStruct((RING**2, 2, rows, other), BF)
+    *first, second = each_result(add_first_kernel, place, pieces, [one] * RING + [many])
+    left = "".join(name for name in AXES if name != PARTS[1][2][0])
+    second = lax.all_to_all(second, axes_of(left), 0, 0, tiled=True)
+    one = jax.ShapeDtypeStruct((2, rows, width), BF)
+    first = each_result(add_second_kernel, place, to_shifts(1, first), [one] * RING)
+    whole_result = jax.ShapeDtypeStruct((2, rows, PARTS[1][1]), BF)
+    (results,) = each_result(
+        add_last_kernel, place, to_shifts(2, first) + [second], [whole_result]
+    )
+    return results
 
 
 def over_core(x):
@@ -422,7 +454,10 @@
     gate_blocks = transposed(gate_weight)
     up_blocks, down_blocks = transposed(up_weight), transposed(down_weight)
     gate_cols = to_owners(gate_blocks)
-    gate_cols, up_blocks, down_blocks = together(gate_cols, up_blocks, down_blocks)
+    merged_attention = average(attention_out[0])
+    gate_cols, up_blocks, down_blocks, merged_attention = together(
+        gate_cols, up_blocks, down_blocks, merged_attention
+    )
     their_gate = over_core(half_blocks(gate_cols, 1 - core))
     up_cols = to_owners(up_blocks)
     up_cols, down_blocks = together(up_cols, down_blocks)
@@ -442,8 +477,7 @@
     hidden, gate_delta, up_delta, by_token = expert(
         core_id, mine, theirs, gate_cols, up_cols, down_cols, slot_gate, spread
     )
-    their_token, attention = together(over_core(by_token), attention_out[0])
-    merged_attention = average(attention)
+    their_token = over_core(by_token)
     place = jnp.stack(
         [core, 2 * lax.axis_index("xh") + lax.axis_index("xl"), lax.axis_index("z"), lax.axis_index("y")]
     ).astype(jnp.int32)
@@ -454,13 +488,13 @@
         (gate_cols, up_cols, down_cols),
         (their_gate, their_up, their_down),
     )
-    got = exchanged(0, pieces)
+    got = to_shifts(0, pieces[:RING])
+    got.append(lax.all_to_all(pieces[RING], axes_of(PARTS[1][2][0]), 0, 0, tiled=True))
     gate_grads, up_grads = weight_grads(core_id, mine, theirs, 0, [gate_delta, up_delta])
     (down_grads,) = weight_grads(core_id, mine, theirs, 1, [hidden])
     *got, gate_grads, up_grads, down_grads = together(*got, gate_grads, up_grads, down_grads)
-    got = exchanged(1, add_pieces(1, place, got))
-    got = exchanged(2, add_pieces(2, place, got))
-    mixed_out, token_grads = add_pieces(3, place, got)
+    results = reduced(place, got)
+    mixed_out, token_grads = results[0], results[1]
     return (
         merged_attention,
         mixed_out,

time: 352 us -> 350 us (level)
  local copies, waits for them, and re-layouts: 11.1 us -> 15.2 us
    all_to_all x2, waiting for transfers between devices: 75.2 us -> 38.1 us  [to_owners(): return lax.all_to_all(blocks, FSDP, 0, 0, tiled=True)]
    ppermute x3, waiting for transfers between devices: 4.26 us -> 34.1 us  [average(): total = total + lax.ppermute(sent, BRANCH, there).astype(F32)]
    all_to_all x0 -> x2, starting transfers between devices: none -> 14.1 us  [the longest x1 9.28 us: reduced(): second = lax.all_to_all(second, axes_of(left), 0, 0, tiled=True)]
    ppermute x18 -> x9, starting transfers between devices: 24.6 us -> 14.2 us  [to_shifts(): got.append(lax.ppermute(piece, axes_of(PARTS[0][2][stage]), there))]
    ppermute x18 -> x9, waiting for transfers between devices: 35.5 us -> 43.8 us  [to_shifts(): got.append(lax.ppermute(piece, axes_of(PARTS[0][2][stage]), there))]
    all_gather x1, waiting for transfers between devices: 4.42 us -> 0.01 us  [on_device(): gathered = lax.all_gather(both, PLANE, axis=0, tiled=True)]
  transfers between devices with their start and end apart: 29 -> 22, of which waited for: 15 -> 13; matrix products, arithmetic and copies ran while one was open for 3% -> 3% of each run, Pallas kernels for 10% -> 10%
where the time goes in v3:
time: 350 us; the launch traced here: 348 us
  waiting for transfers between devices  124 us (35%)
  Pallas kernels  88.9 us (25%)
  starting transfers between devices  48 us (14%)
  blocking collectives  47.3 us (14%)
  local copies, waits for them, and re-layouts  15.2 us (4%)
  between operations  14.3 us (4%)
  other arithmetic  10.4 us (3%)
    all_to_all x1, blocking collectives, to_owners(): return lax.all_to_all(blocks, FSDP, 0, 0, tiled=True)  47.3 us
    ppermute x9, waiting for transfers between devices, to_shifts(): got.append(lax.ppermute(piece, axes_of(PARTS[0][2][stage]), there))  43.8 us
    all_to_all x2, waiting for transfers between devices, to_owners(): return lax.all_to_all(blocks, FSDP, 0, 0, tiled=True)  38.1 us
    ppermute x3, waiting for transfers between devices, average(): total = total + lax.ppermute(sent, BRANCH, there).astype(F32)  34.1 us
    pallas_call x1, Pallas kernels, first_pieces(): call(sums_kernel, 1, (2, 2), [whole(mine.shape)] * 2 + [pl.BlockSpec((per...  21.6 us
    pallas_call x1, Pallas kernels, expert(): call(expert_kernel, 1, (2, 2), row_specs(0, total, width) + row_specs(1,...  17.8 us
    pallas_call x2, Pallas kernels, weight_grads(): call(weight_grad_kernel, 1, (2, 2), rows + [whole(d.shape) for d in delta...  14.7 us
    all_to_all x2, starting transfers between devices, to_owners(): return lax.all_to_all(blocks, FSDP, 0, 0, tiled=True)  14.7 us
  transfers between devices with their start and end apart: 22, of which 13 were waited for; matrix products, arithmetic and copies ran while one was open for 3% of the time, Pallas kernels for 10%

profile of v3, /device:TPU:1, one launch (start us, length us, event | category | flops | bytes accessed | tf_op | source)
XLA Modules:
  0.0 347.7 jit_solution(4878733224449194939)
XLA Ops:
  10.2 3.3 transpose_weight.3
  13.6 9.8 %all-to-all-start = ((bf16[32,344,128]{2,1,0:T(8,128)(2,1)}), bf16[32,344,128]{2,1,0:T(8,128)(2,1)S(1)}, u32[]{:S(2)}, u32[]{:S(2)}) async-start(bf16[32,344,128]{2,1,0:T(8,128)(2,1)} %bitcast.48), calls=%async_computation | async-start | bytes 5636096 | tf_op jit(solution)/shard_map/all_to_all | solution.py:66
  23.5 2.0 dynamic-slice_bitcast_fusion.2
  25.4 3.3 collective-permute-start
  29.3 3.3 transpose_weight.4
  32.6 3.3 transpose_weight.5
  35.9 24.3 %collective-permute-done = bf16[128,1024]{1,0:T(8,128)(2,1)S(1)} collective-permute-done((bf16[128,1024]{1,0:T(8,128)(2,1)}, bf16[128,1024]{1,0:T(8,128)(2,1)S(1)}, u32[]{:S(2)}, u32[]{:S(2)}) %collective-permute-start) | collective-permute-done | bytes 262176 | tf_op jit(solution)/shard_map/ppermute | solution.py:433
  60.2 8.6 %collective-permute-done.1 = bf16[128,1024]{1,0:T(8,128)(2,1)} collective-permute-done((bf16[128,1024]{1,0:T(8,128)(2,1)}, bf16[128,1024]{1,0:T(8,128)(2,1)}, u32[]{:S(2)}, u32[]{:S(2)}) %collective-permute-start.1) | collective-permute-done | bytes 262176 | tf_op jit(solution)/shard_map/ppermute | solution.py:433
  70.0 2.0 fusion.6
  72.0 47.3 %all_to_all.25.up_cols.up = bf16[32,344,128]{2,1,0:T(8,128)(2,1)} all-to-all(bf16[32,344,128]{2,1,0:T(8,128)(2,1)} %bitcast.50), channel_id=1, replica_groups=mesh['xh'=2,'c'=2,'xl'=2,'z'=4,'y'=4] {'xl','z','y'}, dimensions={0} | all-to-all | bytes 5636096 | tf_op jit(solution)/shard_map/all_to_all | solution.py:66
  119.2 4.9 %all-to-all-start.2 = ((bf16[32,344,128]{2,1,0:T(8,128)(2,1)}), bf16[32,344,128]{2,1,0:T(8,128)(2,1)}, u32[]{:S(2)}, u32[]{:S(2)}) async-start(bf16[32,344,128]{2,1,0:T(8,128)(2,1)} %bitcast.49), calls=%async_computation.2 | async-start | bytes 5636096 | tf_op jit(solution)/shard_map/all_to_all | solution.py:66
  128.7 1.9 collective-permute-done.4.their_up
  130.6 38.1 %all-to-all-done.2.down_cols.down = bf16[32,344,128]{2,1,0:T(8,128)(2,1)} async-done(((bf16[32,344,128]{2,1,0:T(8,128)(2,1)}), bf16[32,344,128]{2,1,0:T(8,128)(2,1)}, u32[]{:S(2)}, u32[]{:S(2)}) %all-to-all-start.2) | async-done | bytes 2818080 | tf_op jit(solution)/shard_map/all_to_all | solution.py:66
  173.7 6.8 %pick_rows.3 = bf16[2,2,576,1024]{3,2,1,0:T(8,128)(2,1)} custom-call(bf16[4,144,256]{2,1,0:T(8,128)(2,1)} %fusion.1.sel_ref, f32[576,1]{1,0:T(8,128)} %reshape.231.gate_ref, bf16[2,4,256,2176]{3,2,1,0:T(8,128)(2,1)} %bitcast.44), custom_call_target="tpu_custom_call" | custom-call | flops 1 | bytes 1 | tf_op jit(solution)/shard_map/pick_rows/pallas_call | solution.py:86
  184.7 6.9 %pick_rows.2.mine_in.mine_grad.mine = bf16[2,2,576,1024]{3,2,1,0:T(8,128)(2,1)} custom-call(bf16[4,144,256]{2,1,0:T(8,128)(2,1)} %fusion.2.sel_ref, f32[576,1]{1,0:T(8,128)} %reshape.230.gate_ref.slot_gate, bf16[2,4,256,2176]{3,2,1,0:T(8,128)(2,1)} %bitcast.45), custom_call_target="tpu_custom_call" | custom-call | flops 1 | bytes 1 | tf_op jit(solution)/shard_map/pick_rows/pallas_call | solution.py:86
  192.6 17.8 %expert.1 = (bf16[576,344]{1,0:T(8,128)(2,1)}, bf16[576,344]{1,0:T(8,128)(2,1)}, bf16[576,344]{1,0:T(8,128)(2,1)}, bf16[3,1024,384]{2,1,0:T(8,128)(2,1)}) custom-call(s32[1]{0:T(128)} %bitcast.7.core_ref, bf16[2,2,576,1024]{3,2,1,0:T(8,128)(2,1)} %pick_rows.2.mine_in.mine_grad.mine, ...), custom_call_target="tpu_custom_call" | custom-call | flops 1 | bytes 1 | tf_op jit(solution)/shard_map/expert/pallas_call | solution.py:167
  211.4 3.9 %collective-permute-done.7.theirs = bf16[3,1024,384]{2,1,0:T(8,128)(2,1)S(1)} collective-permute-done((bf16[3,1024,384]{2,1,0:T(8,128)(2,1)}, bf16[3,1024,384]{2,1,0:T(8,128)(2,1)S(1)}, u32[]{:S(2)}, u32[]{:S(2)}) %collective-permute-start.7) | collective-permute-done | bytes 2359328 | tf_op jit(solution)/shard_map/ppermute | solution.py:379
  216.7 21.6 %token_sums.1 = (bf16[2,16,32,512]{3,2,1,0:T(8,128)(2,1)}, bf16[2,16,32,512]{3,2,1,0:T(8,128)(2,1)}, bf16[2,16,32,512]{3,2,1,0:T(8,128)(2,1)}, bf16[2,16,32,512]...) custom-call(s32[4]{0:T(128)} %pad_add_fusion.place_ref, bf16[3,1024,384]{2,1,0:T(8,128)(2,1)} %get-tuple-element.57.mine, ...), custom_call_target="tpu_custom_call" | custom-call | flops 1 | bytes 1 | tf_op jit(solution)/shard_map/token_sums/pallas_call | solution.py:284
  238.3 4.9 %all-to-all-start.3 = ((bf16[4,2,16,32,512]{4,3,2,1,0:T(8,128)(2,1)}), bf16[4,2,16,32,512]{4,3,2,1,0:T(8,128)(2,1)}, u32[]{:S(2)}, u32[]{:S(2)}) async-start(bf16[4,2,16,32,512]{4,3,2,1,0:T(8,128)(2,1)} %get-tuple-element.65), calls=%async_computation.3 | async-start | bytes 8388608 | tf_op jit(solution)/shard_map/all_to_all | solution.py:492
  243.2 3.2 collective-permute-start.10
  246.4 2.7 collective-permute-start.9
  249.1 6.4 %weight_grads.3 = bf16[344,4096]{1,0:T(8,128)(2,1)} custom-call(s32[1]{0:T(128)} %bitcast.7.core_ref, bf16[2,2,576,1024]{3,2,1,0:T(8,128)(2,1)} %pick_rows.2.mine_in.mine_grad.mine, bf16[2,2,576,1024]{3,2,1,0:T(8,128)(2,1)} %collective-permute-done.5.theirs_in.theirs_grad.theirs, bf16[576,344]{1,0:T(8,128)(2,1)} %get-tuple-element.70.refs_0_), custom_call_target="tpu_custom_call" | custom-call | flops 1 | bytes 1 | tf_op jit(solution)/shard_map/weight_grads/pallas_call | solution.py:198
  255.5 8.3 %weight_grads.2 = (bf16[344,4096]{1,0:T(8,128)(2,1)}, bf16[344,4096]{1,0:T(8,128)(2,1)}) custom-call(s32[1]{0:T(128)} %bitcast.7.core_ref, bf16[2,2,576,1024]{3,2,1,0:T(8,128)(2,1)} %pick_rows.2.mine_in.mine_grad.mine, bf16[2,2,576,1024]{3,2,1,0:T(8,128)(2,1)} %collective-permute-done.5.theirs_in.theirs_grad.theirs, ...), custom_call_target="tpu_custom_call" | custom-call | flops 1 | bytes 1 | tf_op jit(solution)/shard_map/weight_grads/pallas_call | solution.py:198
  263.8 6.1 %collective-permute-done.10.refs_3_ = bf16[2,16,32,512]{3,2,1,0:T(8,128)(2,1)S(1)} collective-permute-done((bf16[2,16,32,512]{3,2,1,0:T(8,128)(2,1)}, bf16[2,16,32,512]{3,2,1,0:T(8,128)(2,1)S(1)}, u32[]{:S(2)}, u32[]{:S(2)}) %collective-permute-start.10) | collective-permute-done | bytes 1048608 | tf_op jit(solution)/shard_map/ppermute | solution.py:357
  269.9 22.8 %collective-permute-done.8.refs_1_ = bf16[2,16,32,512]{3,2,1,0:T(8,128)(2,1)S(1)} collective-permute-done((bf16[2,16,32,512]{3,2,1,0:T(8,128)(2,1)}, bf16[2,16,32,512]{3,2,1,0:T(8,128)(2,1)S(1)}, u32[]{:S(2)}, u32[]{:S(2)}) %collective-permute-start.8) | collective-permute-done | bytes 1048608 | tf_op jit(solution)/shard_map/ppermute | solution.py:357
  294.1 5.6 %add_pieces.3 = (bf16[2,4,32,512]{3,2,1,0:T(8,128)(2,1)}, bf16[2,4,32,512]{3,2,1,0:T(8,128)(2,1)}, bf16[2,4,32,512]{3,2,1,0:T(8,128)(2,1)}, bf16[2,4,32,512]{3,2,1,0:T(8,128)(2,1)}, bf16[16,2,32,512]{3,2,1,0:T(8,128)(2,1)}) custom-call(s32[4]{0:T(128)} %pad_add_fusion.place_ref, bf16[2,16,32,512]{3,2,1,0:T(8,128)(2,1)} %get-tuple-element.71.refs_0_, ...), custom_call_target="tpu_custom_call" | custom-call | flops 1 | bytes 1 | tf_op jit(solution)/shard_map/add_pieces/pallas_call | solution.py:338
  299.7 9.3 %all-to-all-start.4 = ((bf16[16,2,32,512]{3,2,1,0:T(8,128)(2,1)}), bf16[16,2,32,512]{3,2,1,0:T(8,128)(2,1)S(1)}, u32[]{:S(2)}, u32[]{:S(2)}) async-start(bf16[16,2,32,512]{3,2,1,0:T(8,128)(2,1)} %get-tuple-element.84), calls=%async_computation.4 | async-start | bytes 2097152 | tf_op jit(solution)/shard_map/all_to_all | solution.py:368
  313.3 4.3 %collective-permute-done.11.refs_1_ = bf16[2,4,32,512]{3,2,1,0:T(8,128)(2,1)S(1)} collective-permute-done((bf16[2,4,32,512]{3,2,1,0:T(8,128)(2,1)}, bf16[2,4,32,512]{3,2,1,0:T(8,128)(2,1)S(1)}, u32[]{:S(2)}, u32[]{:S(2)}) %collective-permute-start.11) | collective-permute-done | bytes 262176 | tf_op jit(solution)/shard_map/ppermute | solution.py:357
  317.6 6.5 %collective-permute-done.13.refs_3_ = bf16[2,4,32,512]{3,2,1,0:T(8,128)(2,1)S(1)} collective-permute-done((bf16[2,4,32,512]{3,2,1,0:T(8,128)(2,1)}, bf16[2,4,32,512]{3,2,1,0:T(8,128)(2,1)S(1)}, u32[]{:S(2)}, u32[]{:S(2)}) %collective-permute-start.13) | collective-permute-done | bytes 262176 | tf_op jit(solution)/shard_map/ppermute | solution.py:357
  324.8 2.6 add_pieces.4
  332.1 3.5 %collective-permute-done.16.refs_3_ = bf16[2,32,512]{2,1,0:T(8,128)(2,1)S(1)} collective-permute-done((bf16[2,32,512]{2,1,0:T(8,128)(2,1)}, bf16[2,32,512]{2,1,0:T(8,128)(2,1)S(1)}, u32[]{:S(2)}, u32[]{:S(2)}) %collective-permute-start.16) | collective-permute-done | bytes 65568 | tf_op jit(solution)/shard_map/ppermute | solution.py:357
  336.6 2.7 add_pieces.5
  (97 shorter events, 35.2 us)
Async XLA Ops:
  7.2 161.6 %all-gather.2.cloned.1.call-start = ((), (), s32[]{:S(2)}) async-start(), calls=%async_computation.5 | async-start | bytes 9052160 | tf_op jit(solution)/shard_map/all_gather | solution.py:451
  13.6 58.4 %all-to-all-start = ((bf16[32,344,128]{2,1,0:T(8,128)(2,1)}), bf16[32,344,128]{2,1,0:T(8,128)(2,1)S(1)}, u32[]{:S(2)}, u32[]{:S(2)}) async-start(bf16[32,344,128]{2,1,0:T(8,128)(2,1)} %bitcast.48), calls=%async_computation | async-start | bytes 5636096 | tf_op jit(solution)/shard_map/all_to_all | solution.py:66
  25.4 34.8 %collective-permute-start = (bf16[128,1024]{1,0:T(8,128)(2,1)}, bf16[128,1024]{1,0:T(8,128)(2,1)S(1)}, u32[]{:S(2)}, u32[]{:S(2)}) collective-permute-start(bf16[128,1024]{1,0:T(8,128)(2,1)} %get-tuple-element.93), channel_id=1, source_target_pairs={{0,32},{32,64},{64,96},{96,0},{1,33},{33,65},{65,97},{97,1},{2,34}... | collective-permute-start | bytes 786440 | tf_op jit(solution)/shard_map/ppermute | solution.py:433
  28.7 40.1 %collective-permute-start.1 = (bf16[128,1024]{1,0:T(8,128)(2,1)}, bf16[128,1024]{1,0:T(8,128)(2,1)}, u32[]{:S(2)}, u32[]{:S(2)}) collective-permute-start(bf16[128,1024]{1,0:T(8,128)(2,1)} %get-tuple-element.95), channel_id=1, source_target_pairs={{0,64},{32,96},{64,0},{96,32},{1,65},{33,97},{65,1},{97,33},{2,66}... | collective-permute-start | bytes 786440 | tf_op jit(solution)/shard_map/ppermute | solution.py:433
  29.3 40.7 %collective-permute-start.2 = (bf16[128,1024]{1,0:T(8,128)(2,1)S(1)}, bf16[128,1024]{1,0:T(8,128)(2,1)}, u32[]{:S(2)}, u32[]{:S(2)}) collective-permute-start(bf16[128,1024]{1,0:T(8,128)(2,1)S(1)} %get-tuple-element.94), channel_id=1, source_target_pairs={{0,96},{32,0},{64,32},{96,64},{1,97},{33,1},{65,33},{97,65},{2,98}... | collective-permute-start | bytes 786440 | tf_op jit(solution)/shard_map/ppermute | solution.py:433
  72.0 52.2 %copy-start = (bf16[32,344,128]{2,1,0:T(8,128)(2,1)}, bf16[32,344,128]{2,1,0:T(8,128)(2,1)S(1)}, u32[]{:S(2)}) copy-start(bf16[32,344,128]{2,1,0:T(8,128)(2,1)S(1)} %all-to-all-done.gate_cols.gate) | copy-start | bytes 8454148
  119.2 49.5 %all-to-all-start.2 = ((bf16[32,344,128]{2,1,0:T(8,128)(2,1)}), bf16[32,344,128]{2,1,0:T(8,128)(2,1)}, u32[]{:S(2)}, u32[]{:S(2)}) async-start(bf16[32,344,128]{2,1,0:T(8,128)(2,1)} %bitcast.49), calls=%async_computation.2 | async-start | bytes 5636096 | tf_op jit(solution)/shard_map/all_to_all | solution.py:66
  124.1 2.4 copy-start.1
  125.3 3.4 collective-permute-start.3
  126.6 4.1 %collective-permute-start.4 = (bf16[16,344,128]{2,1,0:T(8,128)(2,1)S(1)}, bf16[16,344,128]{2,1,0:T(8,128)(2,1)}, u32[]{:S(2)}, u32[]{:S(2)}) collective-permute-start(bf16[16,344,128]{2,1,0:T(8,128)(2,1)S(1)} %bitcast.52), channel_id=1, source_target_pairs={{0,32},{32,0},{1,33},{33,1},{2,34},{34,2},{3,35},{35,3},{4,36},{36... | collective-permute-start | bytes 4227080 | tf_op jit(solution)/shard_map/ppermute | solution.py:379
  128.7 51.8 %copy-start.4 = (bf16[16,344,128]{2,1,0:T(8,128)(2,1)}, bf16[16,344,128]{2,1,0:T(8,128)(2,1)S(1)}, u32[]{:S(2)}) copy-start(bf16[16,344,128]{2,1,0:T(8,128)(2,1)S(1)} %collective-permute-done.3.their_gate) | copy-start | bytes 4227076
  180.5 12.1 %collective-permute-start.5 = (bf16[2,2,576,1024]{3,2,1,0:T(8,128)(2,1)}, bf16[2,2,576,1024]{3,2,1,0:T(8,128)(2,1)}, u32[]{:S(2)}, u32[]{:S(2)}) collective-permute-start(bf16[2,2,576,1024]{3,2,1,0:T(8,128)(2,1)} %pick_rows.3), channel_id=1, source_target_pairs={{0,32},{32,0},{1,33},{33,1},{2,34},{34,2},{3,35},{35,3},{4,36},{36... | collective-permute-start | bytes 14155784 | tf_op jit(solution)/shard_map/ppermute | solution.py:379
  182.2 10.4 %collective-permute-start.6 = (bf16[16,344,128]{2,1,0:T(8,128)(2,1)S(1)}, bf16[16,344,128]{2,1,0:T(8,128)(2,1)S(1)}, u32[]{:S(2)}, u32[]{:S(2)}) collective-permute-start(bf16[16,344,128]{2,1,0:T(8,128)(2,1)S(1)} %bitcast.53), channel_id=1, source_target_pairs={{0,32},{32,0},{1,33},{33,1},{2,34},{34,2},{3,35},{35,3},{4,36},{36... | collective-permute-start | bytes 4227080 | tf_op jit(solution)/shard_map/ppermute | solution.py:379
  192.6 17.9 %copy-start.5 = (bf16[16,344,128]{2,1,0:T(8,128)(2,1)}, bf16[16,344,128]{2,1,0:T(8,128)(2,1)S(1)}, u32[]{:S(2)}) copy-start(bf16[16,344,128]{2,1,0:T(8,128)(2,1)S(1)} %collective-permute-done.6.their_down) | copy-start | bytes 4227076
  210.4 4.8 %collective-permute-start.7 = (bf16[3,1024,384]{2,1,0:T(8,128)(2,1)}, bf16[3,1024,384]{2,1,0:T(8,128)(2,1)S(1)}, u32[]{:S(2)}, u32[]{:S(2)}) collective-permute-start(bf16[3,1024,384]{2,1,0:T(8,128)(2,1)} %get-tuple-element.57.mine), channel_id=1, source_target_pairs={{0,32},{32,0},{1,33},{33,1},{2,34},{34,2},{3,35},{35,3},{4,36},{36... | collective-permute-start | bytes 7077896 | tf_op jit(solution)/shard_map/ppermute | solution.py:379
  215.3 1.4 copy-start.3
  238.3 54.4 %all-to-all-start.3 = ((bf16[4,2,16,32,512]{4,3,2,1,0:T(8,128)(2,1)}), bf16[4,2,16,32,512]{4,3,2,1,0:T(8,128)(2,1)}, u32[]{:S(2)}, u32[]{:S(2)}) async-start(bf16[4,2,16,32,512]{4,3,2,1,0:T(8,128)(2,1)} %get-tuple-element.65), calls=%async_computation.3 | async-start | bytes 8388608 | tf_op jit(solution)/shard_map/all_to_all | solution.py:492
  243.2 26.7 %collective-permute-start.10 = (bf16[2,16,32,512]{3,2,1,0:T(8,128)(2,1)}, bf16[2,16,32,512]{3,2,1,0:T(8,128)(2,1)S(1)}, u32[]{:S(2)}, u32[]{:S(2)}) collective-permute-start(bf16[2,16,32,512]{3,2,1,0:T(8,128)(2,1)} %get-tuple-element.64), channel_id=1, source_target_pairs={{0,64},{16,80},{64,0},{80,16},{1,65},{17,81},{65,1},{81,17},{2,66}... | collective-permute-start | bytes 3145736 | tf_op jit(solution)/shard_map/ppermute | solution.py:357
  246.4 46.3 %collective-permute-start.8 = (bf16[2,16,32,512]{3,2,1,0:T(8,128)(2,1)}, bf16[2,16,32,512]{3,2,1,0:T(8,128)(2,1)S(1)}, u32[]{:S(2)}, u32[]{:S(2)}) collective-permute-start(bf16[2,16,32,512]{3,2,1,0:T(8,128)(2,1)} %get-tuple-element.62), channel_id=1, source_target_pairs={{0,16},{16,64},{64,80},{80,0},{1,17},{17,65},{65,81},{81,1},{2,18}... | collective-permute-start | bytes 3145736 | tf_op jit(solution)/shard_map/ppermute | solution.py:357
  246.4 46.3 %collective-permute-start.9 = (bf16[2,16,32,512]{3,2,1,0:T(8,128)(2,1)}, bf16[2,16,32,512]{3,2,1,0:T(8,128)(2,1)S(1)}, u32[]{:S(2)}, u32[]{:S(2)}) collective-permute-start(bf16[2,16,32,512]{3,2,1,0:T(8,128)(2,1)} %get-tuple-element.63), channel_id=1, source_target_pairs={{0,80},{16,0},{64,16},{80,64},{1,81},{17,1},{65,17},{81,65},{2,82}... | collective-permute-start | bytes 3145736 | tf_op jit(solution)/shard_map/ppermute | solution.py:357
  269.9 22.8 %copy-start.6 = (bf16[2,16,32,512]{3,2,1,0:T(8,128)(2,1)}, bf16[2,16,32,512]{3,2,1,0:T(8,128)(2,1)S(1)}, u32[]{:S(2)}) copy-start(bf16[2,16,32,512]{3,2,1,0:T(8,128)(2,1)S(1)} %collective-permute-done.10.refs_3_) | copy-start | bytes 3145732
  299.7 35.9 %all-to-all-start.4 = ((bf16[16,2,32,512]{3,2,1,0:T(8,128)(2,1)}), bf16[16,2,32,512]{3,2,1,0:T(8,128)(2,1)S(1)}, u32[]{:S(2)}, u32[]{:S(2)}) async-start(bf16[16,2,32,512]{3,2,1,0:T(8,128)(2,1)} %get-tuple-element.84), calls=%async_computation.4 | async-start | bytes 2097152 | tf_op jit(solution)/shard_map/all_to_all | solution.py:368
  309.0 8.6 %collective-permute-start.11 = (bf16[2,4,32,512]{3,2,1,0:T(8,128)(2,1)}, bf16[2,4,32,512]{3,2,1,0:T(8,128)(2,1)S(1)}, u32[]{:S(2)}, u32[]{:S(2)}) collective-permute-start(bf16[2,4,32,512]{3,2,1,0:T(8,128)(2,1)} %get-tuple-element.77), channel_id=1, source_target_pairs={{0,4},{4,8},{8,12},{12,0},{1,5},{5,9},{9,13},{13,1},{2,6},{6,10},{... | collective-permute-start | bytes 786440 | tf_op jit(solution)/shard_map/ppermute | solution.py:357
  310.3 7.3 %collective-permute-start.12 = (bf16[2,4,32,512]{3,2,1,0:T(8,128)(2,1)}, bf16[2,4,32,512]{3,2,1,0:T(8,128)(2,1)S(1)}, u32[]{:S(2)}, u32[]{:S(2)}) collective-permute-start(bf16[2,4,32,512]{3,2,1,0:T(8,128)(2,1)} %get-tuple-element.78), channel_id=1, source_target_pairs={{0,12},{4,0},{8,4},{12,8},{1,13},{5,1},{9,5},{13,9},{2,14},{6,2},{... | collective-permute-start | bytes 786440 | tf_op jit(solution)/shard_map/ppermute | solution.py:357
  311.7 12.4 %collective-permute-start.13 = (bf16[2,4,32,512]{3,2,1,0:T(8,128)(2,1)}, bf16[2,4,32,512]{3,2,1,0:T(8,128)(2,1)S(1)}, u32[]{:S(2)}, u32[]{:S(2)}) collective-permute-start(bf16[2,4,32,512]{3,2,1,0:T(8,128)(2,1)} %get-tuple-element.79), channel_id=1, source_target_pairs={{0,8},{4,12},{8,0},{12,4},{1,9},{5,13},{9,1},{13,5},{2,10},{6,14},... | collective-permute-start | bytes 786440 | tf_op jit(solution)/shard_map/ppermute | solution.py:357
  317.6 6.5 %copy-start.9 = (bf16[2,4,32,512]{3,2,1,0:T(8,128)(2,1)}, bf16[2,4,32,512]{3,2,1,0:T(8,128)(2,1)S(1)}, u32[]{:S(2)}) copy-start(bf16[2,4,32,512]{3,2,1,0:T(8,128)(2,1)S(1)} %collective-permute-done.11.refs_1_) | copy-start | bytes 786436
  317.6 6.5 %copy-start.10 = (bf16[2,4,32,512]{3,2,1,0:T(8,128)(2,1)}, bf16[2,4,32,512]{3,2,1,0:T(8,128)(2,1)S(1)}, u32[]{:S(2)}) copy-start(bf16[2,4,32,512]{3,2,1,0:T(8,128)(2,1)S(1)} %collective-permute-done.12.refs_2_) | copy-start | bytes 786436
  327.5 4.6 %collective-permute-start.14 = (bf16[2,32,512]{2,1,0:T(8,128)(2,1)}, bf16[2,32,512]{2,1,0:T(8,128)(2,1)S(1)}, u32[]{:S(2)}, u32[]{:S(2)}) collective-permute-start(bf16[2,32,512]{2,1,0:T(8,128)(2,1)} %get-tuple-element.81), channel_id=1, source_target_pairs={{0,1},{1,2},{2,3},{3,0},{4,5},{5,6},{6,7},{7,4},{8,9},{9,10},{10,1... | collective-permute-start | bytes 196616 | tf_op jit(solution)/shard_map/ppermute | solution.py:357
  328.5 3.6 %collective-permute-start.15 = (bf16[2,32,512]{2,1,0:T(8,128)(2,1)}, bf16[2,32,512]{2,1,0:T(8,128)(2,1)S(1)}, u32[]{:S(2)}, u32[]{:S(2)}) collective-permute-start(bf16[2,32,512]{2,1,0:T(8,128)(2,1)} %get-tuple-element.82), channel_id=1, source_target_pairs={{0,3},{1,0},{2,1},{3,2},{4,7},{5,4},{6,5},{7,6},{8,11},{9,8},{10,9... | collective-permute-start | bytes 196616 | tf_op jit(solution)/shard_map/ppermute | solution.py:357
  330.2 5.4 %collective-permute-start.16 = (bf16[2,32,512]{2,1,0:T(8,128)(2,1)}, bf16[2,32,512]{2,1,0:T(8,128)(2,1)S(1)}, u32[]{:S(2)}, u32[]{:S(2)}) collective-permute-start(bf16[2,32,512]{2,1,0:T(8,128)(2,1)} %get-tuple-element.83), channel_id=1, source_target_pairs={{0,2},{1,3},{2,0},{3,1},{4,6},{5,7},{6,4},{7,5},{8,10},{9,11},{10,... | collective-permute-start | bytes 196616 | tf_op jit(solution)/shard_map/ppermute | solution.py:357
  332.1 3.5 %copy-start.12 = (bf16[2,32,512]{2,1,0:T(8,128)(2,1)}, bf16[2,32,512]{2,1,0:T(8,128)(2,1)S(1)}, u32[]{:S(2)}) copy-start(bf16[2,32,512]{2,1,0:T(8,128)(2,1)S(1)} %collective-permute-done.14.refs_1_) | copy-start | bytes 196612
  332.1 3.5 %copy-start.13 = (bf16[2,32,512]{2,1,0:T(8,128)(2,1)}, bf16[2,32,512]{2,1,0:T(8,128)(2,1)S(1)}, u32[]{:S(2)}) copy-start(bf16[2,32,512]{2,1,0:T(8,128)(2,1)S(1)} %collective-permute-done.15.refs_2_) | copy-start | bytes 196612
  (5 other events, 4.6 us)
Sparse Core Ops, SparseCore 0:
  10.9 153.6 all-gather.1

commit v4 on v3

--- a/solution.py
+++ b/solution.py
@@ -321,10 +321,11 @@
 
 
 def add_last_kernel(place_ref, *refs):
-    pieces, second, out = refs[:RING], refs[RING], refs[RING + 1]
+    pieces, second, outs = refs[:RING], refs[RING], refs[RING + 1 :]
     (low, middle, _), (_, high, _) = PARTS
-    out[0, :, low:middle] = added([ref[0] for ref in pieces])
-    out[0, :, middle:high] = added([second[i, 0] for i in range(second.shape[0])])
+    for t, out in enumerate(outs):
+        out[:, low:middle] = added([ref[t] for ref in pieces])
+        out[:, middle:high] = added([second[i, t] for i in range(second.shape[0])])
 
 
 def each_result(kernel, place, arrays, shapes):
@@ -368,11 +369,17 @@
     second = lax.all_to_all(second, axes_of(left), 0, 0, tiled=True)
     one = jax.ShapeDtypeStruct((2, rows, width), BF)
     first = each_result(add_second_kernel, place, to_shifts(1, first), [one] * RING)
-    whole_result = jax.ShapeDtypeStruct((2, rows, PARTS[1][1]), BF)
-    (results,) = each_result(
-        add_last_kernel, place, to_shifts(2, first) + [second], [whole_result]
-    )
-    return results
+    arrays = to_shifts(2, first) + [second]
+    result = jax.ShapeDtypeStruct((rows, PARTS[1][1]), BF)
+    return call(
+        add_last_kernel,
+        1,
+        (1,),
+        [whole(array.shape) for array in arrays],
+        [whole(result.shape)] * 2,
+        [result] * 2,
+        "add_last",
+    )(place, *arrays)
 
 
 def over_core(x):
@@ -493,8 +500,7 @@
     gate_grads, up_grads = weight_grads(core_id, mine, theirs, 0, [gate_delta, up_delta])
     (down_grads,) = weight_grads(core_id, mine, theirs, 1, [hidden])
     *got, gate_grads, up_grads, down_grads = together(*got, gate_grads, up_grads, down_grads)
-    results = reduced(place, got)
-    mixed_out, token_grads = results[0], results[1]
+    mixed_out, token_grads = reduced(place, got)
     return (
         merged_attention,
         mixed_out,

time: 350 us -> 349 us (level)
    pallas_call x3 -> x2, Pallas kernels: 11 us -> 8.29 us  [each_result(): call(kernel, 1, (2,), [spec(array.shape, i >= RING) for i, array in enume...]
where the time goes in v4:
time: 349 us; the launch traced here: 346 us
  waiting for transfers between devices  124 us (36%)
  Pallas kernels  89 us (26%)
  starting transfers between devices  48 us (14%)
  blocking collectives  47.3 us (14%)
  between operations  14.3 us (4%)
  local copies, waits for them, and re-layouts  13.6 us (4%)
  other arithmetic  10.4 us (3%)
    all_to_all x1, blocking collectives, to_owners(): return lax.all_to_all(blocks, FSDP, 0, 0, tiled=True)  47.3 us
    ppermute x9, waiting for transfers between devices, to_shifts(): got.append(lax.ppermute(piece, axes_of(PARTS[0][2][stage]), there))  43.8 us
    all_to_all x2, waiting for transfers between devices, to_owners(): return lax.all_to_all(blocks, FSDP, 0, 0, tiled=True)  38.1 us
    ppermute x3, waiting for transfers between devices, average(): total = total + lax.ppermute(sent, BRANCH, there).astype(F32)  34.1 us
    pallas_call x1, Pallas kernels, first_pieces(): call(sums_kernel, 1, (2, 2), [whole(mine.shape)] * 2 + [pl.BlockSpec((per...  21.6 us
    pallas_call x1, Pallas kernels, expert(): call(expert_kernel, 1, (2, 2), row_specs(0, total, width) + row_specs(1,...  17.8 us
    pallas_call x2, Pallas kernels, weight_grads(): call(weight_grad_kernel, 1, (2, 2), rows + [whole(d.shape) for d in delta...  14.7 us
    all_to_all x2, starting transfers between devices, to_owners(): return lax.all_to_all(blocks, FSDP, 0, 0, tiled=True)  14.7 us
  transfers between devices with their start and end apart: 22, of which 13 were waited for; matrix products, arithmetic and copies ran while one was open for 3% of the time, Pallas kernels for 10%

profile of v4, /device:TPU:1, one launch (start us, length us, event | category | flops | bytes accessed | tf_op | source)
XLA Modules:
  0.0 346.2 jit_solution(10412672816011827837)
XLA Ops:
  10.2 3.3 transpose_weight.3
  13.6 9.8 %all-to-all-start = ((bf16[32,344,128]{2,1,0:T(8,128)(2,1)}), bf16[32,344,128]{2,1,0:T(8,128)(2,1)S(1)}, u32[]{:S(2)}, u32[]{:S(2)}) async-start(bf16[32,344,128]{2,1,0:T(8,128)(2,1)} %bitcast.44), calls=%async_computation | async-start | bytes 5636096 | tf_op jit(solution)/shard_map/all_to_all | solution.py:66
  23.5 2.0 dynamic-slice_bitcast_fusion.2
  25.4 3.3 collective-permute-start
  29.3 3.3 transpose_weight.4
  32.6 3.3 transpose_weight.5
  35.9 24.3 %collective-permute-done = bf16[128,1024]{1,0:T(8,128)(2,1)S(1)} collective-permute-done((bf16[128,1024]{1,0:T(8,128)(2,1)}, bf16[128,1024]{1,0:T(8,128)(2,1)S(1)}, u32[]{:S(2)}, u32[]{:S(2)}) %collective-permute-start) | collective-permute-done | bytes 262176 | tf_op jit(solution)/shard_map/ppermute | solution.py:440
  60.2 8.6 %collective-permute-done.1 = bf16[128,1024]{1,0:T(8,128)(2,1)} collective-permute-done((bf16[128,1024]{1,0:T(8,128)(2,1)}, bf16[128,1024]{1,0:T(8,128)(2,1)}, u32[]{:S(2)}, u32[]{:S(2)}) %collective-permute-start.1) | collective-permute-done | bytes 262176 | tf_op jit(solution)/shard_map/ppermute | solution.py:440
  70.0 2.0 fusion.6
  72.0 47.3 %all_to_all.25.up_cols.up = bf16[32,344,128]{2,1,0:T(8,128)(2,1)} all-to-all(bf16[32,344,128]{2,1,0:T(8,128)(2,1)} %bitcast.46), channel_id=1, replica_groups=mesh['xh'=2,'c'=2,'xl'=2,'z'=4,'y'=4] {'xl','z','y'}, dimensions={0} | all-to-all | bytes 5636096 | tf_op jit(solution)/shard_map/all_to_all | solution.py:66
  119.2 4.9 %all-to-all-start.2 = ((bf16[32,344,128]{2,1,0:T(8,128)(2,1)}), bf16[32,344,128]{2,1,0:T(8,128)(2,1)}, u32[]{:S(2)}, u32[]{:S(2)}) async-start(bf16[32,344,128]{2,1,0:T(8,128)(2,1)} %bitcast.45), calls=%async_computation.2 | async-start | bytes 5636096 | tf_op jit(solution)/shard_map/all_to_all | solution.py:66
  128.7 1.9 collective-permute-done.4.their_up
  130.6 38.1 %all-to-all-done.2.down_cols.down = bf16[32,344,128]{2,1,0:T(8,128)(2,1)} async-done(((bf16[32,344,128]{2,1,0:T(8,128)(2,1)}), bf16[32,344,128]{2,1,0:T(8,128)(2,1)}, u32[]{:S(2)}, u32[]{:S(2)}) %all-to-all-start.2) | async-done | bytes 2818080 | tf_op jit(solution)/shard_map/all_to_all | solution.py:66
  173.7 6.8 %pick_rows.3 = bf16[2,2,576,1024]{3,2,1,0:T(8,128)(2,1)} custom-call(bf16[4,144,256]{2,1,0:T(8,128)(2,1)} %fusion.1.sel_ref, f32[576,1]{1,0:T(8,128)} %reshape.231.gate_ref, bf16[2,4,256,2176]{3,2,1,0:T(8,128)(2,1)} %bitcast.40), custom_call_target="tpu_custom_call" | custom-call | flops 1 | bytes 1 | tf_op jit(solution)/shard_map/pick_rows/pallas_call | solution.py:86
  184.7 6.9 %pick_rows.2.mine_in.mine_grad.mine = bf16[2,2,576,1024]{3,2,1,0:T(8,128)(2,1)} custom-call(bf16[4,144,256]{2,1,0:T(8,128)(2,1)} %fusion.2.sel_ref, f32[576,1]{1,0:T(8,128)} %reshape.230.gate_ref.slot_gate, bf16[2,4,256,2176]{3,2,1,0:T(8,128)(2,1)} %bitcast.41), custom_call_target="tpu_custom_call" | custom-call | flops 1 | bytes 1 | tf_op jit(solution)/shard_map/pick_rows/pallas_call | solution.py:86
  192.6 17.8 %expert.1 = (bf16[576,344]{1,0:T(8,128)(2,1)}, bf16[576,344]{1,0:T(8,128)(2,1)}, bf16[576,344]{1,0:T(8,128)(2,1)}, bf16[3,1024,384]{2,1,0:T(8,128)(2,1)}) custom-call(s32[1]{0:T(128)} %bitcast.7.core_ref, bf16[2,2,576,1024]{3,2,1,0:T(8,128)(2,1)} %pick_rows.2.mine_in.mine_grad.mine, ...), custom_call_target="tpu_custom_call" | custom-call | flops 1 | bytes 1 | tf_op jit(solution)/shard_map/expert/pallas_call | solution.py:167
  211.4 3.9 %collective-permute-done.7.theirs = bf16[3,1024,384]{2,1,0:T(8,128)(2,1)S(1)} collective-permute-done((bf16[3,1024,384]{2,1,0:T(8,128)(2,1)}, bf16[3,1024,384]{2,1,0:T(8,128)(2,1)S(1)}, u32[]{:S(2)}, u32[]{:S(2)}) %collective-permute-start.7) | collective-permute-done | bytes 2359328 | tf_op jit(solution)/shard_map/ppermute | solution.py:386
  216.7 21.6 %token_sums.1 = (bf16[2,16,32,512]{3,2,1,0:T(8,128)(2,1)}, bf16[2,16,32,512]{3,2,1,0:T(8,128)(2,1)}, bf16[2,16,32,512]{3,2,1,0:T(8,128)(2,1)}, bf16[2,16,32,512]...) custom-call(s32[4]{0:T(128)} %pad_add_fusion.place_ref, bf16[3,1024,384]{2,1,0:T(8,128)(2,1)} %get-tuple-element.59.mine, ...), custom_call_target="tpu_custom_call" | custom-call | flops 1 | bytes 1 | tf_op jit(solution)/shard_map/token_sums/pallas_call | solution.py:284
  238.3 4.9 %all-to-all-start.3 = ((bf16[4,2,16,32,512]{4,3,2,1,0:T(8,128)(2,1)}), bf16[4,2,16,32,512]{4,3,2,1,0:T(8,128)(2,1)}, u32[]{:S(2)}, u32[]{:S(2)}) async-start(bf16[4,2,16,32,512]{4,3,2,1,0:T(8,128)(2,1)} %get-tuple-element.67), calls=%async_computation.3 | async-start | bytes 8388608 | tf_op jit(solution)/shard_map/all_to_all | solution.py:499
  243.2 3.2 collective-permute-start.10
  246.4 2.7 collective-permute-start.9
  249.1 6.4 %weight_grads.3 = bf16[344,4096]{1,0:T(8,128)(2,1)} custom-call(s32[1]{0:T(128)} %bitcast.7.core_ref, bf16[2,2,576,1024]{3,2,1,0:T(8,128)(2,1)} %pick_rows.2.mine_in.mine_grad.mine, bf16[2,2,576,1024]{3,2,1,0:T(8,128)(2,1)} %collective-permute-done.5.theirs_in.theirs_grad.theirs, bf16[576,344]{1,0:T(8,128)(2,1)} %get-tuple-element.72.refs_0_), custom_call_target="tpu_custom_call" | custom-call | flops 1 | bytes 1 | tf_op jit(solution)/shard_map/weight_grads/pallas_call | solution.py:198
  255.5 8.3 %weight_grads.2 = (bf16[344,4096]{1,0:T(8,128)(2,1)}, bf16[344,4096]{1,0:T(8,128)(2,1)}) custom-call(s32[1]{0:T(128)} %bitcast.7.core_ref, bf16[2,2,576,1024]{3,2,1,0:T(8,128)(2,1)} %pick_rows.2.mine_in.mine_grad.mine, bf16[2,2,576,1024]{3,2,1,0:T(8,128)(2,1)} %collective-permute-done.5.theirs_in.theirs_grad.theirs, ...), custom_call_target="tpu_custom_call" | custom-call | flops 1 | bytes 1 | tf_op jit(solution)/shard_map/weight_grads/pallas_call | solution.py:198
  263.8 6.1 %collective-permute-done.10.refs_3_ = bf16[2,16,32,512]{3,2,1,0:T(8,128)(2,1)S(1)} collective-permute-done((bf16[2,16,32,512]{3,2,1,0:T(8,128)(2,1)}, bf16[2,16,32,512]{3,2,1,0:T(8,128)(2,1)S(1)}, u32[]{:S(2)}, u32[]{:S(2)}) %collective-permute-start.10) | collective-permute-done | bytes 1048608 | tf_op jit(solution)/shard_map/ppermute | solution.py:358
  269.9 22.8 %collective-permute-done.8.refs_1_ = bf16[2,16,32,512]{3,2,1,0:T(8,128)(2,1)S(1)} collective-permute-done((bf16[2,16,32,512]{3,2,1,0:T(8,128)(2,1)}, bf16[2,16,32,512]{3,2,1,0:T(8,128)(2,1)S(1)}, u32[]{:S(2)}, u32[]{:S(2)}) %collective-permute-start.8) | collective-permute-done | bytes 1048608 | tf_op jit(solution)/shard_map/ppermute | solution.py:358
  294.1 5.6 %add_pieces.2 = (bf16[2,4,32,512]{3,2,1,0:T(8,128)(2,1)}, bf16[2,4,32,512]{3,2,1,0:T(8,128)(2,1)}, bf16[2,4,32,512]{3,2,1,0:T(8,128)(2,1)}, bf16[2,4,32,512]{3,2,1,0:T(8,128)(2,1)}, bf16[16,2,32,512]{3,2,1,0:T(8,128)(2,1)}) custom-call(s32[4]{0:T(128)} %pad_add_fusion.place_ref, bf16[2,16,32,512]{3,2,1,0:T(8,128)(2,1)} %get-tuple-element.73.refs_0_, ...), custom_call_target="tpu_custom_call" | custom-call | flops 1 | bytes 1 | tf_op jit(solution)/shard_map/add_pieces/pallas_call | solution.py:339
  299.7 9.3 %all-to-all-start.4 = ((bf16[16,2,32,512]{3,2,1,0:T(8,128)(2,1)}), bf16[16,2,32,512]{3,2,1,0:T(8,128)(2,1)S(1)}, u32[]{:S(2)}, u32[]{:S(2)}) async-start(bf16[16,2,32,512]{3,2,1,0:T(8,128)(2,1)} %get-tuple-element.86), calls=%async_computation.4 | async-start | bytes 2097152 | tf_op jit(solution)/shard_map/all_to_all | solution.py:369
  313.3 4.3 %collective-permute-done.11.refs_1_ = bf16[2,4,32,512]{3,2,1,0:T(8,128)(2,1)S(1)} collective-permute-done((bf16[2,4,32,512]{3,2,1,0:T(8,128)(2,1)}, bf16[2,4,32,512]{3,2,1,0:T(8,128)(2,1)S(1)}, u32[]{:S(2)}, u32[]{:S(2)}) %collective-permute-start.11) | collective-permute-done | bytes 262176 | tf_op jit(solution)/shard_map/ppermute | solution.py:358
  317.6 6.5 %collective-permute-done.13.refs_3_ = bf16[2,4,32,512]{3,2,1,0:T(8,128)(2,1)S(1)} collective-permute-done((bf16[2,4,32,512]{3,2,1,0:T(8,128)(2,1)}, bf16[2,4,32,512]{3,2,1,0:T(8,128)(2,1)S(1)}, u32[]{:S(2)}, u32[]{:S(2)}) %collective-permute-start.13) | collective-permute-done | bytes 262176 | tf_op jit(solution)/shard_map/ppermute | solution.py:358
  324.8 2.6 add_pieces.3
  332.1 3.5 %collective-permute-done.16.refs_3_ = bf16[2,32,512]{2,1,0:T(8,128)(2,1)S(1)} collective-permute-done((bf16[2,32,512]{2,1,0:T(8,128)(2,1)}, bf16[2,32,512]{2,1,0:T(8,128)(2,1)S(1)}, u32[]{:S(2)}, u32[]{:S(2)}) %collective-permute-start.16) | collective-permute-done | bytes 65568 | tf_op jit(solution)/shard_map/ppermute | solution.py:358
  336.6 2.8 add_last.1
  (96 shorter events, 33.6 us)
Async XLA Ops:
  7.2 161.6 %all-gather.2.cloned.1.call-start = ((), (), s32[]{:S(2)}) async-start(), calls=%async_computation.5 | async-start | bytes 9052160 | tf_op jit(solution)/shard_map/all_gather | solution.py:458
  13.6 58.4 %all-to-all-start = ((bf16[32,344,128]{2,1,0:T(8,128)(2,1)}), bf16[32,344,128]{2,1,0:T(8,128)(2,1)S(1)}, u32[]{:S(2)}, u32[]{:S(2)}) async-start(bf16[32,344,128]{2,1,0:T(8,128)(2,1)} %bitcast.44), calls=%async_computation | async-start | bytes 5636096 | tf_op jit(solution)/shard_map/all_to_all | solution.py:66
  25.4 34.8 %collective-permute-start = (bf16[128,1024]{1,0:T(8,128)(2,1)}, bf16[128,1024]{1,0:T(8,128)(2,1)S(1)}, u32[]{:S(2)}, u32[]{:S(2)}) collective-permute-start(bf16[128,1024]{1,0:T(8,128)(2,1)} %get-tuple-element.97), channel_id=1, source_target_pairs={{0,32},{32,64},{64,96},{96,0},{1,33},{33,65},{65,97},{97,1},{2,34}... | collective-permute-start | bytes 786440 | tf_op jit(solution)/shard_map/ppermute | solution.py:440
  28.7 40.1 %collective-permute-start.1 = (bf16[128,1024]{1,0:T(8,128)(2,1)}, bf16[128,1024]{1,0:T(8,128)(2,1)}, u32[]{:S(2)}, u32[]{:S(2)}) collective-permute-start(bf16[128,1024]{1,0:T(8,128)(2,1)} %get-tuple-element.99), channel_id=1, source_target_pairs={{0,64},{32,96},{64,0},{96,32},{1,65},{33,97},{65,1},{97,33},{2,66}... | collective-permute-start | bytes 786440 | tf_op jit(solution)/shard_map/ppermute | solution.py:440
  29.3 40.7 %collective-permute-start.2 = (bf16[128,1024]{1,0:T(8,128)(2,1)S(1)}, bf16[128,1024]{1,0:T(8,128)(2,1)}, u32[]{:S(2)}, u32[]{:S(2)}) collective-permute-start(bf16[128,1024]{1,0:T(8,128)(2,1)S(1)} %get-tuple-element.98), channel_id=1, source_target_pairs={{0,96},{32,0},{64,32},{96,64},{1,97},{33,1},{65,33},{97,65},{2,98}... | collective-permute-start | bytes 786440 | tf_op jit(solution)/shard_map/ppermute | solution.py:440
  72.0 52.2 %copy-start = (bf16[32,344,128]{2,1,0:T(8,128)(2,1)}, bf16[32,344,128]{2,1,0:T(8,128)(2,1)S(1)}, u32[]{:S(2)}) copy-start(bf16[32,344,128]{2,1,0:T(8,128)(2,1)S(1)} %all-to-all-done.gate_cols.gate) | copy-start | bytes 8454148
  119.2 49.5 %all-to-all-start.2 = ((bf16[32,344,128]{2,1,0:T(8,128)(2,1)}), bf16[32,344,128]{2,1,0:T(8,128)(2,1)}, u32[]{:S(2)}, u32[]{:S(2)}) async-start(bf16[32,344,128]{2,1,0:T(8,128)(2,1)} %bitcast.45), calls=%async_computation.2 | async-start | bytes 5636096 | tf_op jit(solution)/shard_map/all_to_all | solution.py:66
  124.1 2.4 copy-start.1
  125.3 3.4 collective-permute-start.3
  126.6 4.1 %collective-permute-start.4 = (bf16[16,344,128]{2,1,0:T(8,128)(2,1)S(1)}, bf16[16,344,128]{2,1,0:T(8,128)(2,1)}, u32[]{:S(2)}, u32[]{:S(2)}) collective-permute-start(bf16[16,344,128]{2,1,0:T(8,128)(2,1)S(1)} %bitcast.48), channel_id=1, source_target_pairs={{0,32},{32,0},{1,33},{33,1},{2,34},{34,2},{3,35},{35,3},{4,36},{36... | collective-permute-start | bytes 4227080 | tf_op jit(solution)/shard_map/ppermute | solution.py:386
  128.7 51.8 %copy-start.4 = (bf16[16,344,128]{2,1,0:T(8,128)(2,1)}, bf16[16,344,128]{2,1,0:T(8,128)(2,1)S(1)}, u32[]{:S(2)}) copy-start(bf16[16,344,128]{2,1,0:T(8,128)(2,1)S(1)} %collective-permute-done.3.their_gate) | copy-start | bytes 4227076
  180.5 12.1 %collective-permute-start.5 = (bf16[2,2,576,1024]{3,2,1,0:T(8,128)(2,1)}, bf16[2,2,576,1024]{3,2,1,0:T(8,128)(2,1)}, u32[]{:S(2)}, u32[]{:S(2)}) collective-permute-start(bf16[2,2,576,1024]{3,2,1,0:T(8,128)(2,1)} %pick_rows.3), channel_id=1, source_target_pairs={{0,32},{32,0},{1,33},{33,1},{2,34},{34,2},{3,35},{35,3},{4,36},{36... | collective-permute-start | bytes 14155784 | tf_op jit(solution)/shard_map/ppermute | solution.py:386
  182.2 10.4 %collective-permute-start.6 = (bf16[16,344,128]{2,1,0:T(8,128)(2,1)S(1)}, bf16[16,344,128]{2,1,0:T(8,128)(2,1)S(1)}, u32[]{:S(2)}, u32[]{:S(2)}) collective-permute-start(bf16[16,344,128]{2,1,0:T(8,128)(2,1)S(1)} %bitcast.49), channel_id=1, source_target_pairs={{0,32},{32,0},{1,33},{33,1},{2,34},{34,2},{3,35},{35,3},{4,36},{36... | collective-permute-start | bytes 4227080 | tf_op jit(solution)/shard_map/ppermute | solution.py:386
  192.6 17.9 %copy-start.5 = (bf16[16,344,128]{2,1,0:T(8,128)(2,1)}, bf16[16,344,128]{2,1,0:T(8,128)(2,1)S(1)}, u32[]{:S(2)}) copy-start(bf16[16,344,128]{2,1,0:T(8,128)(2,1)S(1)} %collective-permute-done.6.their_down) | copy-start | bytes 4227076
  210.4 4.8 %collective-permute-start.7 = (bf16[3,1024,384]{2,1,0:T(8,128)(2,1)}, bf16[3,1024,384]{2,1,0:T(8,128)(2,1)S(1)}, u32[]{:S(2)}, u32[]{:S(2)}) collective-permute-start(bf16[3,1024,384]{2,1,0:T(8,128)(2,1)} %get-tuple-element.59.mine), channel_id=1, source_target_pairs={{0,32},{32,0},{1,33},{33,1},{2,34},{34,2},{3,35},{35,3},{4,36},{36... | collective-permute-start | bytes 7077896 | tf_op jit(solution)/shard_map/ppermute | solution.py:386
  215.3 1.4 copy-start.3
  238.3 54.4 %all-to-all-start.3 = ((bf16[4,2,16,32,512]{4,3,2,1,0:T(8,128)(2,1)}), bf16[4,2,16,32,512]{4,3,2,1,0:T(8,128)(2,1)}, u32[]{:S(2)}, u32[]{:S(2)}) async-start(bf16[4,2,16,32,512]{4,3,2,1,0:T(8,128)(2,1)} %get-tuple-element.67), calls=%async_computation.3 | async-start | bytes 8388608 | tf_op jit(solution)/shard_map/all_to_all | solution.py:499
  243.2 26.7 %collective-permute-start.10 = (bf16[2,16,32,512]{3,2,1,0:T(8,128)(2,1)}, bf16[2,16,32,512]{3,2,1,0:T(8,128)(2,1)S(1)}, u32[]{:S(2)}, u32[]{:S(2)}) collective-permute-start(bf16[2,16,32,512]{3,2,1,0:T(8,128)(2,1)} %get-tuple-element.66), channel_id=1, source_target_pairs={{0,64},{16,80},{64,0},{80,16},{1,65},{17,81},{65,1},{81,17},{2,66}... | collective-permute-start | bytes 3145736 | tf_op jit(solution)/shard_map/ppermute | solution.py:358
  246.4 46.3 %collective-permute-start.8 = (bf16[2,16,32,512]{3,2,1,0:T(8,128)(2,1)}, bf16[2,16,32,512]{3,2,1,0:T(8,128)(2,1)S(1)}, u32[]{:S(2)}, u32[]{:S(2)}) collective-permute-start(bf16[2,16,32,512]{3,2,1,0:T(8,128)(2,1)} %get-tuple-element.64), channel_id=1, source_target_pairs={{0,16},{16,64},{64,80},{80,0},{1,17},{17,65},{65,81},{81,1},{2,18}... | collective-permute-start | bytes 3145736 | tf_op jit(solution)/shard_map/ppermute | solution.py:358
  246.4 46.3 %collective-permute-start.9 = (bf16[2,16,32,512]{3,2,1,0:T(8,128)(2,1)}, bf16[2,16,32,512]{3,2,1,0:T(8,128)(2,1)S(1)}, u32[]{:S(2)}, u32[]{:S(2)}) collective-permute-start(bf16[2,16,32,512]{3,2,1,0:T(8,128)(2,1)} %get-tuple-element.65), channel_id=1, source_target_pairs={{0,80},{16,0},{64,16},{80,64},{1,81},{17,1},{65,17},{81,65},{2,82}... | collective-permute-start | bytes 3145736 | tf_op jit(solution)/shard_map/ppermute | solution.py:358
  269.9 22.8 %copy-start.6 = (bf16[2,16,32,512]{3,2,1,0:T(8,128)(2,1)}, bf16[2,16,32,512]{3,2,1,0:T(8,128)(2,1)S(1)}, u32[]{:S(2)}) copy-start(bf16[2,16,32,512]{3,2,1,0:T(8,128)(2,1)S(1)} %collective-permute-done.10.refs_3_) | copy-start | bytes 3145732
  299.7 35.9 %all-to-all-start.4 = ((bf16[16,2,32,512]{3,2,1,0:T(8,128)(2,1)}), bf16[16,2,32,512]{3,2,1,0:T(8,128)(2,1)S(1)}, u32[]{:S(2)}, u32[]{:S(2)}) async-start(bf16[16,2,32,512]{3,2,1,0:T(8,128)(2,1)} %get-tuple-element.86), calls=%async_computation.4 | async-start | bytes 2097152 | tf_op jit(solution)/shard_map/all_to_all | solution.py:369
  309.0 8.6 %collective-permute-start.11 = (bf16[2,4,32,512]{3,2,1,0:T(8,128)(2,1)}, bf16[2,4,32,512]{3,2,1,0:T(8,128)(2,1)S(1)}, u32[]{:S(2)}, u32[]{:S(2)}) collective-permute-start(bf16[2,4,32,512]{3,2,1,0:T(8,128)(2,1)} %get-tuple-element.79), channel_id=1, source_target_pairs={{0,4},{4,8},{8,12},{12,0},{1,5},{5,9},{9,13},{13,1},{2,6},{6,10},{... | collective-permute-start | bytes 786440 | tf_op jit(solution)/shard_map/ppermute | solution.py:358
  310.3 7.3 %collective-permute-start.12 = (bf16[2,4,32,512]{3,2,1,0:T(8,128)(2,1)}, bf16[2,4,32,512]{3,2,1,0:T(8,128)(2,1)S(1)}, u32[]{:S(2)}, u32[]{:S(2)}) collective-permute-start(bf16[2,4,32,512]{3,2,1,0:T(8,128)(2,1)} %get-tuple-element.80), channel_id=1, source_target_pairs={{0,12},{4,0},{8,4},{12,8},{1,13},{5,1},{9,5},{13,9},{2,14},{6,2},{... | collective-permute-start | bytes 786440 | tf_op jit(solution)/shard_map/ppermute | solution.py:358
  311.7 12.4 %collective-permute-start.13 = (bf16[2,4,32,512]{3,2,1,0:T(8,128)(2,1)}, bf16[2,4,32,512]{3,2,1,0:T(8,128)(2,1)S(1)}, u32[]{:S(2)}, u32[]{:S(2)}) collective-permute-start(bf16[2,4,32,512]{3,2,1,0:T(8,128)(2,1)} %get-tuple-element.81), channel_id=1, source_target_pairs={{0,8},{4,12},{8,0},{12,4},{1,9},{5,13},{9,1},{13,5},{2,10},{6,14},... | collective-permute-start | bytes 786440 | tf_op jit(solution)/shard_map/ppermute | solution.py:358
  317.6 6.5 %copy-start.9 = (bf16[2,4,32,512]{3,2,1,0:T(8,128)(2,1)}, bf16[2,4,32,512]{3,2,1,0:T(8,128)(2,1)S(1)}, u32[]{:S(2)}) copy-start(bf16[2,4,32,512]{3,2,1,0:T(8,128)(2,1)S(1)} %collective-permute-done.11.refs_1_) | copy-start | bytes 786436
  317.6 6.5 %copy-start.10 = (bf16[2,4,32,512]{3,2,1,0:T(8,128)(2,1)}, bf16[2,4,32,512]{3,2,1,0:T(8,128)(2,1)S(1)}, u32[]{:S(2)}) copy-start(bf16[2,4,32,512]{3,2,1,0:T(8,128)(2,1)S(1)} %collective-permute-done.12.refs_2_) | copy-start | bytes 786436
  327.5 4.6 %collective-permute-start.14 = (bf16[2,32,512]{2,1,0:T(8,128)(2,1)}, bf16[2,32,512]{2,1,0:T(8,128)(2,1)S(1)}, u32[]{:S(2)}, u32[]{:S(2)}) collective-permute-start(bf16[2,32,512]{2,1,0:T(8,128)(2,1)} %get-tuple-element.83), channel_id=1, source_target_pairs={{0,1},{1,2},{2,3},{3,0},{4,5},{5,6},{6,7},{7,4},{8,9},{9,10},{10,1... | collective-permute-start | bytes 196616 | tf_op jit(solution)/shard_map/ppermute | solution.py:358
  328.5 3.6 %collective-permute-start.15 = (bf16[2,32,512]{2,1,0:T(8,128)(2,1)}, bf16[2,32,512]{2,1,0:T(8,128)(2,1)S(1)}, u32[]{:S(2)}, u32[]{:S(2)}) collective-permute-start(bf16[2,32,512]{2,1,0:T(8,128)(2,1)} %get-tuple-element.84), channel_id=1, source_target_pairs={{0,3},{1,0},{2,1},{3,2},{4,7},{5,4},{6,5},{7,6},{8,11},{9,8},{10,9... | collective-permute-start | bytes 196616 | tf_op jit(solution)/shard_map/ppermute | solution.py:358
  330.2 5.4 %collective-permute-start.16 = (bf16[2,32,512]{2,1,0:T(8,128)(2,1)}, bf16[2,32,512]{2,1,0:T(8,128)(2,1)S(1)}, u32[]{:S(2)}, u32[]{:S(2)}) collective-permute-start(bf16[2,32,512]{2,1,0:T(8,128)(2,1)} %get-tuple-element.85), channel_id=1, source_target_pairs={{0,2},{1,3},{2,0},{3,1},{4,6},{5,7},{6,4},{7,5},{8,10},{9,11},{10,... | collective-permute-start | bytes 196616 | tf_op jit(solution)/shard_map/ppermute | solution.py:358
  332.1 3.5 %copy-start.12 = (bf16[2,32,512]{2,1,0:T(8,128)(2,1)}, bf16[2,32,512]{2,1,0:T(8,128)(2,1)S(1)}, u32[]{:S(2)}) copy-start(bf16[2,32,512]{2,1,0:T(8,128)(2,1)S(1)} %collective-permute-done.14.refs_1_) | copy-start | bytes 196612
  332.1 3.5 %copy-start.13 = (bf16[2,32,512]{2,1,0:T(8,128)(2,1)}, bf16[2,32,512]{2,1,0:T(8,128)(2,1)S(1)}, u32[]{:S(2)}) copy-start(bf16[2,32,512]{2,1,0:T(8,128)(2,1)S(1)} %collective-permute-done.15.refs_2_) | copy-start | bytes 196612
  (5 other events, 4.6 us)
Sparse Core Ops, SparseCore 0:
  10.9 153.6 all-gather.1
